TPU v7x, 32 devices: a whole 2x2x4 slice. The times are simulated.
32 devices in a mesh: rows: 8 (over z, y), cols: 4 (over x, core).
Axes of the slice: x: 2, y: 2, z: 4, core: 2. Of those that a mesh axis runs over, the one named last changes fastest.
Arguments:
- prior: bfloat16 [128, 16, 128, 128], P('rows', 'cols'), may hold values from -6 to 6
- candidates: int32 [128, 16], P('rows', 'cols'), may hold values from 0 to 127, as said below
- cross_link: int32 [128], P(('rows', 'cols')), may hold values from 0 to 127, as said below
- a1_blocks: bfloat16 [128, 2, 128, 128], P(('rows', 'cols')), may hold values from -0.375 to 0.375
- a2_blocks: bfloat16 [128, 128, 128], P(('rows', 'cols')), may hold values from -0.5 to 0.5
Outputs:
- similarity: bfloat16 [128, 16, 128, 128], P('rows', 'cols')
Inputs may be any that keep to these rules, and one draw needn't show every extreme that they name: Target block t lies in target slab t // 16 and quarter (t // 4) % 4; a candidate in columns q * 4 to (q + 1) * 4 - 1 names a target of quarter q. The candidates of one row block in one quarter lie in distinct target slabs. Of the candidates held by one device, at most 8 lie in one target slab, and some slab gets exactly 8; every target slab gets 16 * 4 candidates of its quarter from all source slabs together. `cross_link`: the linked row block of a row block in slab r lies in the last half of the row blocks of slab (r + 1) % 8.
All inputs are finite; a program needn't handle non-finite values.
Results may differ from a plain program's by a relative error of at most 0.006.
Values may be sent and summed in bfloat16 or wider, within the bound.
No kernel may reach another device: no remote copies, remote signals or barrier semaphores. Data moves between devices by JAX's collectives and lax.ppermute only.
A program may use at most 64 MiB of HBM per device.

v0:
```python
import jax
import jax.numpy as jnp
from jax import lax
from jax.sharding import PartitionSpec as P

mixing = 0.75


def passed_along(array, axis, by):
    count = lax.axis_size(axis)
    return lax.ppermute(array, axis, [(i, (i + by) % count) for i in range(count)])


def local(prior, candidates, cross_link, a1_blocks, a2_blocks):
    row_blocks = prior.shape[0]
    per_quarter = prior.shape[1]
    block = prior.shape[2]
    targets_here = a2_blocks.shape[0]
    slab_count = lax.axis_size("rows")
    column_count = lax.axis_size("cols")
    capacity = max(1, row_blocks * per_quarter // slab_count)
    upper_half = row_blocks // 2
    adjacency, links = (
        lax.all_gather(a1_blocks, "cols", axis=0, tiled=True),
        lax.all_gather(cross_link, "cols", axis=0, tiled=True),
    )
    within = links % row_blocks - upper_half
    next_ids = passed_along(candidates[upper_half:], "rows", -1)
    neighbour_ids = next_ids[within]
    matches = candidates[:, :, None] == neighbour_ids[:, None, :]
    chosen = jnp.sum(
        jnp.where(matches, jnp.arange(per_quarter, dtype=jnp.int32)[None, None, :], 0), axis=2
    )
    found = jnp.any(matches, axis=2)
    self_blocks = adjacency[:, 0]
    cross_blocks = adjacency[:, 1]

    def left_product(values):
        next_values = passed_along(values[upper_half:], "rows", -1)
        gathered = next_values[within]
        picked = jnp.take_along_axis(gathered, chosen[:, :, None, None], axis=1)
        picked = jnp.where(found[:, :, None, None], picked, jnp.zeros_like(picked))
        own_term = jnp.einsum(
            "ixy,ikyz->ikxz", self_blocks, values, preferred_element_type=jnp.float32
        )
        return own_term + jnp.einsum(
            "ixy,ikyz->ikxz", cross_blocks, picked, preferred_element_type=jnp.float32
        )

    flat_ids = candidates.reshape(-1)
    dest_slab = flat_ids // (column_count * targets_here)
    local_index = flat_ids % targets_here
    onehot = (dest_slab[:, None] == jnp.arange(slab_count, dtype=jnp.int32)[None, :]).astype(
        jnp.int32
    )
    running = jnp.cumsum(onehot, axis=0)
    dest_rank = jnp.sum(running * onehot, axis=1) - 1
    position = dest_slab * capacity + dest_rank
    requests = jnp.zeros((slab_count * capacity,), jnp.int32).at[position].set(local_index)
    wanted = lax.all_to_all(requests, "rows", split_axis=0, concat_axis=0, tiled=True)
    first = left_product(prior).astype(jnp.bfloat16)
    empty = jnp.zeros((slab_count * capacity, block, block), jnp.bfloat16)
    send_first = empty.at[position].set(first.reshape(-1, block, block))
    send_prior = empty.at[position].set(prior.reshape(-1, block, block))
    got_first, got_prior = (
        lax.all_to_all(send_first, "rows", split_axis=0, concat_axis=0, tiled=True),
        lax.all_to_all(send_prior, "rows", split_axis=0, concat_axis=0, tiled=True),
    )
    local_blocks = a2_blocks[wanted]
    image = jnp.einsum("sxy,szy->sxz", got_first, local_blocks, preferred_element_type=jnp.float32)
    swept = (mixing * image + (1.0 - mixing) * got_prior.astype(jnp.float32)).astype(jnp.bfloat16)
    product = jnp.einsum(
        "sxy,szy->sxz", swept, local_blocks, preferred_element_type=jnp.float32
    ).astype(jnp.bfloat16)
    returned = lax.all_to_all(product, "rows", split_axis=0, concat_axis=0, tiled=True)
    carried = returned[position].reshape(row_blocks, per_quarter, block, block)
    second = left_product(carried)
    return (mixing * second + (1.0 - mixing) * prior.astype(jnp.float32)).astype(jnp.bfloat16)


def solution(mesh):
    placed = (
        P("rows", "cols", None, None),
        P("rows", "cols"),
        P(("rows", "cols")),
        P(("rows", "cols"), None, None, None),
        P(("rows", "cols"), None, None),
    )
    return jax.shard_map(
        local, mesh=mesh, in_specs=placed, out_specs=P("rows", "cols", None, None), check_vma=False
    )
```

profile of v0, /device:TPU:10, one launch (start us, length us, event | category | flops | bytes accessed | tf_op | source)
XLA Modules:
  0.0 295.8 jit_solution(1129693353215206226)
XLA Ops:
  6.5 0.9 copy.55
  7.5 0.1 reshape.169
  7.7 0.1 reduce_window_sum.11
  7.8 0.2 select_reduce_fusion
  8.0 0.8 scatter_custom_fusion.1
  8.8 0.7 all_to_all.18
  9.5 6.3 %all-to-all-start.1 = ((s32[8,8,1]{1,2,0:T(1,128)}), s32[8,8,1]{1,2,0:T(1,128)S(1)}, u32[]{:S(2)}, u32[]{:S(2)}) async-start(s32[8,8,1]{1,2,0:T(1,128)} %bitcast.15), calls=%async_computation.1 | async-start | bytes 8192 | tf_op jit(solution)/shard_map/all_to_all | solution.py:60
  15.7 1.8 broadcast_in_dim.35.clone
  17.6 8.6 %scatter_fusion.1 = bf16[64,128,128]{2,1,0:T(8,128)(2,1)} fusion(bf16[64,128,128]{2,1,0:T(8,128)(2,1)} %broadcast_in_dim.35.clone, s32[64]{0:T(128)S(1)} %fusion.14, bf16[64,128,128]{2,1,0:T(8,128)(2,1)S(1)} %bitcast.56), kind=kCustom, calls=%fused_computation.9 | custom fusion | bytes 6291712 | tf_op jit(solution)/shard_map/scatter | solution.py:64
  26.2 6.1 %all-to-all-start.2 = ((bf16[64,128,128]{2,1,0:T(8,128)(2,1)}), bf16[64,128,128]{2,1,0:T(8,128)(2,1)}, u32[]{:S(2)}, u32[]{:S(2)}) async-start(bf16[64,128,128]{2,1,0:T(8,128)(2,1)} %scatter_fusion.1), calls=%async_computation.2 | async-start | bytes 4194304 | tf_op jit(solution)/shard_map/all_to_all | solution.py:67
  32.4 0.7 copy.57
  33.1 1.1 slice.20
  34.2 1.5 collective-permute-start.1
  35.7 0.6 dynamic-slice
  37.0 0.2 dynamic-update-slice
  37.3 4.3 %all-reduce = s32[16]{0:T(128)S(1)} all-reduce(s32[16]{0:T(128)S(1)} %dynamic-update-slice), channel_id=1, replica_groups=mesh['rows'=8,'cols'=4] {'cols'}, use_global_device_ids=true, to_apply=%add | all-reduce | flops 16 | bytes 128
  41.6 46.4 %collective-permute-done = s32[8,4]{1,0:T(8,128)S(1)} collective-permute-done((s32[8,4]{1,0:T(8,128)S(1)}, s32[8,4]{1,0:T(8,128)S(1)}, u32[]{:S(2)}, u32[]{:S(2)}) %collective-permute-start) | collective-permute-done | bytes 160 | tf_op jit(solution)/shard_map/ppermute | solution.py:11
  88.0 0.6 gather_fusion
  88.7 0.1 reshape.270
  88.9 0.1 copy.62
  89.0 0.1 copy.61
  89.1 2.1 gather_fusion.1
  91.2 3.7 %gather_fusion.5 = bf16[64,128,128]{2,1,0:T(8,128)(2,1)} fusion(bf16[16,4,128,128]{3,2,1,0:T(8,128)(2,1)} %gather_fusion.1, s32[64]{0:T(128)S(1)} %reshape.270), kind=kCustom, calls=%fused_computation.clone | custom fusion | bytes 4194816 | tf_op jit(solution)/shard_map/jit(take_along_axis)/gather | solution.py:41
  94.9 3.9 %copy.64 = bf16[16,4,128,128]{2,3,1,0:T(8,128)(2,1)} copy(bf16[16,4,128,128]{3,2,1,0:T(8,128)(2,1)} %bitcast.58) | data formatting | bytes 4194304 | tf_op jit(solution)/shard_map/jit(take_along_axis)/gather | solution.py:41
  98.9 2.0 fusion.10
  100.9 2.1 add_convert_fusion.1
  103.0 4.1 %copy.65 = bf16[64,128,128]{2,1,0:T(8,128)(2,1)} copy(bf16[64,128,128]{1,2,0:T(8,128)(2,1)} %bitcast.59) | data formatting | bytes 4194304 | tf_op jit(solution)/shard_map/reshape | solution.py:63
  107.0 1.8 broadcast_in_dim.35.clone.1
  108.9 10.1 %scatter_fusion = bf16[64,128,128]{2,1,0:T(8,128)(2,1)} fusion(bf16[64,128,128]{2,1,0:T(8,128)(2,1)} %broadcast_in_dim.35.clone.1, s32[64]{0:T(128)S(1)} %fusion.14, bf16[64,128,128]{2,1,0:T(8,128)(2,1)} %copy.65), kind=kCustom, calls=%fused_computation.7 | custom fusion | bytes 6291712 | tf_op jit(solution)/shard_map/scatter | solution.py:63
  119.0 17.4 %all-to-all-start = ((bf16[64,128,128]{2,1,0:T(8,128)(2,1)}), bf16[64,128,128]{2,1,0:T(8,128)(2,1)}, u32[]{:S(2)}, u32[]{:S(2)}) async-start(bf16[64,128,128]{2,1,0:T(8,128)(2,1)} %scatter_fusion), calls=%async_computation | async-start | bytes 4194304 | tf_op jit(solution)/shard_map/all_to_all | solution.py:66
  136.3 0.5 broadcast.263
  136.8 0.7 reduce.3
  137.6 2.1 gather_fusion.2
  139.7 39.5 %all-to-all-done = bf16[64,128,128]{2,1,0:T(8,128)(2,1)} async-done(((bf16[64,128,128]{2,1,0:T(8,128)(2,1)}), bf16[64,128,128]{2,1,0:T(8,128)(2,1)}, u32[]{:S(2)}, u32[]{:S(2)}) %all-to-all-start) | async-done | bytes 2097184 | tf_op jit(solution)/shard_map/all_to_all | solution.py:66
  179.3 7.8 %convolution_convert_fusion = bf16[64,128,128]{2,1,0:T(8,128)(2,1)} fusion(bf16[64,128,128]{2,1,0:T(8,128)(2,1)} %gather_fusion.2, bf16[64,128,128]{2,1,0:T(8,128)(2,1)} %all-to-all-done.2, bf16[64,128,128]{2,1,0:T(8,128)(2,1)} %all-to-all-done), kind=kOutput, calls=%fused_computation.20 | convolution fusion | flops 543162368 | bytes 8388608 | tf_op jit(solution)/shard_map/sxy,szy->sxz/dot_general | solution.py:72
  187.1 8.0 %all-to-all-start.3 = ((bf16[64,128,128]{2,1,0:T(8,128)(2,1)}), bf16[64,128,128]{2,1,0:T(8,128)(2,1)}, u32[]{:S(2)}, u32[]{:S(2)}) async-start(bf16[64,128,128]{2,1,0:T(8,128)(2,1)} %convolution_convert_fusion), calls=%async_computation.3 | async-start | bytes 4194304 | tf_op jit(solution)/shard_map/all_to_all | solution.py:75
  195.2 44.8 %all-to-all-done.3 = bf16[64,128,128]{2,1,0:T(8,128)(2,1)} async-done(((bf16[64,128,128]{2,1,0:T(8,128)(2,1)}), bf16[64,128,128]{2,1,0:T(8,128)(2,1)}, u32[]{:S(2)}, u32[]{:S(2)}) %all-to-all-start.3) | async-done | bytes 2097184 | tf_op jit(solution)/shard_map/all_to_all | solution.py:75
  240.0 3.7 %gather_fusion.3 = bf16[64,128,128]{2,1,0:T(8,128)(2,1)} fusion(bf16[64,128,128]{2,1,0:T(8,128)(2,1)} %all-to-all-done.3, s32[1024]{0:T(1024)S(1)} %pad_clamp_fusion), kind=kCustom, calls=%fused_computation.5 | custom fusion | bytes 4194560 | tf_op jit(solution)/shard_map/gather | solution.py:76
  243.7 2.3 slice.41
  246.0 3.8 %collective-permute-start.2 = (bf16[8,4,128,128]{3,2,1,0:T(8,128)(2,1)}, bf16[8,4,128,128]{3,2,1,0:T(8,128)(2,1)S(1)}, u32[]{:S(2)}, u32[]{:S(2)}) collective-permute-start(bf16[8,4,128,128]{3,2,1,0:T(8,128)(2,1)} %bitcast.20), channel_id=1, source_target_pairs={{0,28},{4,0},{8,4},{12,8},{16,12},{20,16},{24,20},{28,24},{1,29},{... | collective-permute-start | bytes 3145736 | tf_op jit(solution)/shard_map/ppermute | solution.py:11
  249.9 2.6 copy.71
  252.5 4.4 %fusion.9 = f32[16,4,128,128]{3,2,1,0:T(8,128)} fusion(bf16[16,4,128,128]{3,2,1,0:T(8,128)(2,1)} %bitcast.57, bf16[16,2,128,128]{3,2,0,1:T(8,128)(2,1)} %all-gather.2.cloned.1.call-done), kind=kOutput, calls=%fused_computation.27 | convolution fusion | flops 268435456 | bytes 6815744 | tf_op jit(solution)/shard_map/ixy,ikyz->ikxz/dot_general | solution.py:43
  256.9 15.0 %collective-permute-done.2 = bf16[8,4,128,128]{3,2,1,0:T(8,128)(2,1)S(1)} collective-permute-done((bf16[8,4,128,128]{3,2,1,0:T(8,128)(2,1)}, bf16[8,4,128,128]{3,2,1,0:T(8,128)(2,1)S(1)}, u32[]{:S(2)}, u32[]{:S(2)}) %collective-permute-start.2) | collective-permute-done | bytes 1048608 | tf_op jit(solution)/shard_map/ppermute | solution.py:11
  271.8 0.9 gather_fusion.4
  272.8 2.2 gather_fusion.6
  275.0 4.2 %copy.70 = bf16[64,128,128]{1,2,0:T(8,128)(2,1)} copy(bf16[64,128,128]{2,1,0:T(8,128)(2,1)} %gather_fusion.6) | data formatting | bytes 4194304 | tf_op jit(solution)/shard_map/jit(take_along_axis)/gather | solution.py:41
  279.1 5.9 %fusion = bf16[16,4,128,128]{2,3,1,0:T(8,128)(2,1)} fusion(bf16[16,4,128,128]{2,3,1,0:T(8,128)(2,1)} %copy.71, f32[16,4,128,128]{3,2,1,0:T(8,128)} %fusion.9, bf16[16,4,128,128]{2,3,1,0:T(8,128)(2,1)} %bitcast.60, pred[16,4]{1,0:T(8,128)(4,1)S(1)} %copy.62, pred[16,4]{1,0:T(8,128)(4,1)S(1)} %copy.61, bf16[16,2,128,128]{3,2,0,1:T(8,128)(2,1)S(1)} %copy-done.4), kind=kOutput, calls=%fused_computation.11 | convolution fusion | flops 276824064 | bytes 11014144 | tf_op jit(solution)/shard_map/ixy,ikyz->ikxz/dot_general | solution.py:46
  285.1 3.9 %copy.72 = bf16[16,4,128,128]{3,2,1,0:T(8,128)(2,1)} copy(bf16[16,4,128,128]{2,3,1,0:T(8,128)(2,1)} %fusion) | data formatting | bytes 4194304 | tf_op jit(solution)/shard_map/convert_element_type | solution.py:78
  (43 shorter events, 0.7 us)
Async XLA Ops:
  6.5 131.1 %copy-start = (bf16[4,128,128]{2,1,0:T(8,128)(2,1)S(1)}, bf16[4,128,128]{2,1,0:T(8,128)(2,1)}, u32[]{:S(2)}) copy-start(bf16[4,128,128]{2,1,0:T(8,128)(2,1)} %param.11) | copy-start | bytes 393220
  6.5 11.0 %copy-start.1 = (bf16[16,4,128,128]{3,2,1,0:T(8,128)(2,1)S(1)}, bf16[16,4,128,128]{3,2,1,0:T(8,128)(2,1)}, u32[]{:S(2)}) copy-start(bf16[16,4,128,128]{3,2,1,0:T(8,128)(2,1)} %param.7) | copy-start | bytes 6291460
  9.5 16.7 %all-to-all-start.1 = ((s32[8,8,1]{1,2,0:T(1,128)}), s32[8,8,1]{1,2,0:T(1,128)S(1)}, u32[]{:S(2)}, u32[]{:S(2)}) async-start(s32[8,8,1]{1,2,0:T(1,128)} %bitcast.15), calls=%async_computation.1 | async-start | bytes 8192 | tf_op jit(solution)/shard_map/all_to_all | solution.py:60
  26.2 6.2 %copy-start.5 = (bf16[4,2,128,128]{3,2,1,0:T(8,128)(2,1)S(1)}, bf16[4,2,128,128]{3,2,1,0:T(8,128)(2,1)}, u32[]{:S(2)}) copy-start(bf16[4,2,128,128]{3,2,1,0:T(8,128)(2,1)} %param.10) | copy-start | bytes 786436
  26.2 92.8 %all-to-all-start.2 = ((bf16[64,128,128]{2,1,0:T(8,128)(2,1)}), bf16[64,128,128]{2,1,0:T(8,128)(2,1)}, u32[]{:S(2)}, u32[]{:S(2)}) async-start(bf16[64,128,128]{2,1,0:T(8,128)(2,1)} %scatter_fusion.1), calls=%async_computation.2 | async-start | bytes 4194304 | tf_op jit(solution)/shard_map/all_to_all | solution.py:67
  32.3 3.4 %copy-start.8 = (u32[32]{0:T(128)S(1)}, u32[32]{0:T(128)}, u32[]{:S(2)}) copy-start(u32[32]{0:T(128)} %constant.111) | copy-start | bytes 388
  32.3 4.7 %copy-start.7 = (s32[4]{0:T(128)S(1)}, s32[4]{0:T(128)}, u32[]{:S(2)}) copy-start(s32[4]{0:T(128)} %param.9) | copy-start | bytes 52
  32.3 56.3 %copy-start.6 = (s32[16,4]{0,1:T(4,128)S(1)}, s32[16,4]{0,1:T(4,128)}, u32[]{:S(2)}) copy-start(s32[16,4]{0,1:T(4,128)} %param.8) | copy-start | bytes 772
  32.3 66.6 %all-gather.2.cloned.1.call-start = ((), (), s32[]{:S(2)}) async-start(), calls=%async_computation.4 | async-start | bytes 1310720 | tf_op jit(solution)/shard_map/all_gather | solution.py:24
  34.2 54.8 %collective-permute-start.1 = (bf16[8,4,128,128]{3,2,1,0:T(8,128)(2,1)}, bf16[8,4,128,128]{3,2,1,0:T(8,128)(2,1)S(1)}, u32[]{:S(2)}, u32[]{:S(2)}) collective-permute-start(bf16[8,4,128,128]{3,2,1,0:T(8,128)(2,1)} %slice.20), channel_id=1, source_target_pairs={{0,28},{4,0},{8,4},{12,8},{16,12},{20,16},{24,20},{28,24},{1,29},{... | collective-permute-start | bytes 3145736 | tf_op jit(solution)/shard_map/ppermute | solution.py:11
  35.7 52.3 %collective-permute-start = (s32[8,4]{1,0:T(8,128)S(1)}, s32[8,4]{1,0:T(8,128)S(1)}, u32[]{:S(2)}, u32[]{:S(2)}) collective-permute-start(s32[8,4]{1,0:T(8,128)S(1)} %slice.39), channel_id=1, source_target_pairs={{0,28},{4,0},{8,4},{12,8},{16,12},{20,16},{24,20},{28,24},{1,29},{... | collective-permute-start | bytes 392 | tf_op jit(solution)/shard_map/ppermute | solution.py:11
  98.9 2.0 copy-start.2
  98.9 2.0 copy-start.3
  119.0 60.3 %all-to-all-start = ((bf16[64,128,128]{2,1,0:T(8,128)(2,1)}), bf16[64,128,128]{2,1,0:T(8,128)(2,1)}, u32[]{:S(2)}, u32[]{:S(2)}) async-start(bf16[64,128,128]{2,1,0:T(8,128)(2,1)} %scatter_fusion), calls=%async_computation | async-start | bytes 4194304 | tf_op jit(solution)/shard_map/all_to_all | solution.py:66
  187.1 52.9 %all-to-all-start.3 = ((bf16[64,128,128]{2,1,0:T(8,128)(2,1)}), bf16[64,128,128]{2,1,0:T(8,128)(2,1)}, u32[]{:S(2)}, u32[]{:S(2)}) async-start(bf16[64,128,128]{2,1,0:T(8,128)(2,1)} %convolution_convert_fusion), calls=%async_computation.3 | async-start | bytes 4194304 | tf_op jit(solution)/shard_map/all_to_all | solution.py:75
  246.0 25.8 %collective-permute-start.2 = (bf16[8,4,128,128]{3,2,1,0:T(8,128)(2,1)}, bf16[8,4,128,128]{3,2,1,0:T(8,128)(2,1)S(1)}, u32[]{:S(2)}, u32[]{:S(2)}) collective-permute-start(bf16[8,4,128,128]{3,2,1,0:T(8,128)(2,1)} %bitcast.20), channel_id=1, source_target_pairs={{0,28},{4,0},{8,4},{12,8},{16,12},{20,16},{24,20},{28,24},{1,29},{... | collective-permute-start | bytes 3145736 | tf_op jit(solution)/shard_map/ppermute | solution.py:11
  275.0 4.2 %copy-start.4 = (bf16[16,2,128,128]{3,2,0,1:T(8,128)(2,1)S(1)}, bf16[16,2,128,128]{3,2,0,1:T(8,128)(2,1)}, u32[]{:S(2)}) copy-start(bf16[16,2,128,128]{3,2,0,1:T(8,128)(2,1)} %all-gather.2.cloned.1.call-done) | copy-start | bytes 3145732
Sparse Core Ops, SparseCore 0:
  34.7 16.7 all-gather.1
where the time goes:
time: 300 us; the launch traced here: 296 us
  waiting for transfers between devices  146 us (49%)
  local copies, waits for them, and re-layouts  65.1 us (22%)
  starting transfers between devices  43.2 us (14%)
  matrix products  22.2 us (7%)
  between operations  14.2 us (5%)
  blocking collectives  4.27 us (1%)
    ppermute x3, waiting for transfers between devices, passed_along(): lax.ppermute(array, axis, [(i, (i + by) % count) for i in range(count)])  61.4 us
    all_to_all x1, waiting for transfers between devices, local(): lax.all_to_all(product, 'rows', split_axis=0, concat_axis=0, tiled=True)  44.8 us
    all_to_all x1, waiting for transfers between devices, local(): lax.all_to_all(send_first, 'rows', split_axis=0, concat_axis=0, tiled=True)  39.5 us
    all_to_all x1, starting transfers between devices, local(): lax.all_to_all(send_first, 'rows', split_axis=0, concat_axis=0, tiled=True)  17.4 us
    gather x6, local copies, waits for them, and re-layouts, left_product(): picked = jnp.take_along_axis(gathered, chosen[:, :, None, None], axis=1)  14.1 us
    scatter x1, local copies, waits for them, and re-layouts, local(): send_first = empty.at[position].set(first.reshape(-1, block, block))  10.1 us
    scatter x1, local copies, waits for them, and re-layouts, local(): send_prior = empty.at[position].set(prior.reshape(-1, block, block))  8.58 us
    all_to_all x1, starting transfers between devices, local(): lax.all_to_all(product, 'rows', split_axis=0, concat_axis=0, tiled=True)  8.04 us
  transfers between devices with their start and end apart: 8, of which 4 were waited for; matrix products, arithmetic and copies ran while one was open for 18% of the time, Pallas kernels for 0%

commit v1 on v0

v1 whole, which is shorter than its diff:
```python
import functools

import jax
import jax.numpy as jnp
from jax import lax
from jax.experimental import pallas as pl
from jax.experimental.pallas import tpu as pltpu
from jax.sharding import PartitionSpec as P

mixing = 0.75
pad = 16
chunk_count = 2


def bits_of(count):
    return count.bit_length() - 1


def exchange(array, axis, mask):
    count = lax.axis_size(axis)
    return lax.ppermute(array, axis, [(i, i ^ mask) for i in range(count)])


def gathered_place(distance, order):
    place = jnp.zeros_like(distance)
    for step, mask in enumerate(order):
        place = place + jnp.where((distance & mask) != 0, 1 << step, 0)
    return place


def transpose_kernel(src, dst):
    for t in range(src.shape[0]):
        dst[t] = src[t].T


def sweep_kernel(
    chunks, rows, per_quarter, block, half, per_step, own_rows, share_rows, next_rows,
    index, p_own, *refs,
):
    near = refs[:chunks]
    passed = refs[chunks : 2 * chunks]
    far = refs[2 * chunks : 3 * chunks]
    a_ref, t_ref, out_ref, p1, p2, fj, sems = refs[3 * chunks :]
    count = half * per_quarter
    wide = per_quarter * block
    step = pl.program_id(0)
    at_a = 0
    at_b = rows
    at_idx1 = at_b + half
    at_idx2 = at_idx1 + rows * per_quarter
    at_t = at_idx2 + count
    at_even = at_t + rows * per_quarter

    def weights(offset):
        start = pl.multiple_of(offset, pad)
        left = a_ref[pl.ds(start, block), :]
        right = a_ref[pl.ds(pl.multiple_of(start + block, pad), block), :]
        return jnp.concatenate([left, right], axis=1)

    def side(blocks):
        return jnp.concatenate(blocks, axis=1)

    def blk(ref, n):
        return ref[pl.ds(pl.multiple_of(n * block, block), block), :]

    @pl.when(step == 0)
    def _():
        each = count // chunks * block
        zero = jnp.zeros((block, block), jnp.bfloat16)
        for ref in (p1, p2, fj):
            ref[pl.ds(count * block, block), :] = zero

        def copies(sources, c, target, sem):
            return pltpu.make_async_copy(
                sources[c].at[pl.ds(0, each), :], target.at[pl.ds(c * each, each), :], sem
            )

        even = index[at_even] == 1

        @pl.when(even)
        def _():
            for c in range(chunks):
                copies(near, c, p1, sems.at[0, c]).start()

        @pl.when(jnp.logical_not(even))
        def _():
            for c in range(chunks):
                copies(passed, c, p1, sems.at[0, c]).start()

        for c in range(chunks):
            copies(far, c, p2, sems.at[1, c]).start()
        for c in range(chunks):
            copies(near, c, p1, sems.at[0, c]).wait()
            copies(far, c, p2, sems.at[1, c]).wait()
        for j in range(half):
            w = weights(index[at_b + j])
            top = side([blk(p1, j * per_quarter + k) for k in range(per_quarter)])
            low = side([blk(p2, index[at_idx2 + j * per_quarter + k]) for k in range(per_quarter)])
            got = jnp.dot(w, jnp.concatenate([top, low], axis=0), preferred_element_type=jnp.float32)
            got = got.astype(jnp.bfloat16)
            for k in range(per_quarter):
                fj[pl.ds((j * per_quarter + k) * block, block), :] = got[:, k * block : (k + 1) * block]

    for u in range(per_step):
        i = step * per_step + u
        w = weights(index[at_a + i])
        picks = [index[at_idx1 + i * per_quarter + k] for k in range(per_quarter)]
        own = side([p_own[u, k] for k in range(per_quarter)])
        cross = side([blk(p1, n) for n in picks])
        first = jnp.dot(w, jnp.concatenate([own, cross], axis=0), preferred_element_type=jnp.float32)
        cross2 = side([blk(fj, n) for n in picks])
        second = jnp.dot(
            w,
            jnp.concatenate([first.astype(jnp.bfloat16), cross2], axis=0),
            preferred_element_type=jnp.float32,
        ).astype(jnp.bfloat16)
        for k in range(per_quarter):
            cut = slice(k * block, (k + 1) * block)
            t = t_ref[index[at_t + i * per_quarter + k]]
            image = jnp.dot(second[:, cut], t, preferred_element_type=jnp.float32)
            swept = (mixing * image + (1.0 - mixing) * first[:, cut]).astype(jnp.bfloat16)
            last = jnp.dot(swept, t, preferred_element_type=jnp.float32)
            out_ref[u, k] = (
                mixing * last + (1.0 - mixing) * p_own[u, k].astype(jnp.float32)
            ).astype(jnp.bfloat16)


def tile_of(values):
    return jnp.pad(values.astype(jnp.bfloat16)[None, :], ((0, pad - 1), (0, 128 - values.shape[0])))


def local(prior, candidates, cross_link, a1_blocks, a2_blocks):
    rows, per_quarter, block = prior.shape[:3]
    here = a2_blocks.shape[0]
    slabs = lax.axis_size("rows")
    quarters = lax.axis_size("cols")
    slab = lax.axis_index("rows")
    quarter = lax.axis_index("cols")
    half = rows // 2
    share = a1_blocks.shape[0]
    part = share // 2
    chunks = chunk_count
    each = half // chunks
    count = half * per_quarter

    target_slab = candidates // (quarters * here)
    target_local = candidates % here
    codes = target_slab * here + target_local
    id_tile = tile_of(
        jnp.concatenate([target_slab[half:].reshape(-1), target_local[half:].reshape(-1)])
    )
    sent = []
    for c in range(chunks):
        piece = prior[half + c * each : half + (c + 1) * each].reshape(-1, block)
        sent.append(jnp.concatenate([piece, id_tile], axis=0) if c == 0 else piece)
    links = cross_link % rows - half
    own_weights = jnp.concatenate([a1_blocks.reshape(-1, block), tile_of(links)], axis=0)
    parts = [
        jnp.concatenate(
            [a1_blocks[c * part : (c + 1) * part].reshape(-1, block), tile_of(links[c * part : (c + 1) * part])],
            axis=0,
        )
        for c in range(2)
    ]

    by_two = [(i, (i - 2) % slabs) for i in range(slabs)]
    to_even = [(i + 1, i) for i in range(0, slabs, 2)]
    to_odd = [(i, i + 1) for i in range(0, slabs, 2)]
    far = [lax.ppermute(x, "rows", by_two) for x in sent]
    near = [lax.ppermute(x, "rows", to_even) for x in sent]
    passed = [lax.ppermute(x, "rows", to_odd) for x in far]

    both = ("rows", "cols")
    upper = range(quarters // 2, quarters)
    kept = [(((s + 1) % slabs) * quarters + q, s * quarters + q) for s in range(slabs) for q in upper]
    moved = [
        (((s + 1) % slabs) * quarters + q, s * quarters + q - quarters // 2)
        for s in range(slabs)
        for q in upper
    ]
    next_part = jnp.where(
        quarter >= quarters // 2,
        lax.ppermute(parts[0], both, kept),
        lax.ppermute(parts[1], both, moved),
    )
    weights = jnp.concatenate([own_weights, next_part], axis=0)
    own_rows, next_rows = own_weights.shape[0], next_part.shape[0]
    share_rows = own_rows + next_rows
    column_order = [1 << b for b in reversed(range(bits_of(quarters)))]
    for mask in column_order:
        weights = jnp.concatenate([weights, exchange(weights, "cols", mask)], axis=0)

    targets = pl.pallas_call(
        transpose_kernel, out_shape=jax.ShapeDtypeStruct(a2_blocks.shape, a2_blocks.dtype)
    )(a2_blocks)
    row_order = [1 << b for b in range(1, bits_of(slabs))] + [1]
    for mask in row_order:
        targets = jnp.concatenate([targets, exchange(targets, "rows", mask)], axis=0)

    def codes_in(buffer):
        values = buffer[-pad, : 2 * count].astype(jnp.int32)
        return (values[:count] * here + values[count:]).reshape(half, per_quarter)

    even = slab % 2 == 0
    codes_far = codes_in(far[0])
    codes_near = jnp.where(even, codes_in(near[0]), codes_in(passed[0]))
    tiles = weights.reshape(quarters, share_rows, block)
    row_quarter = jnp.arange(quarters, dtype=jnp.int32)
    place = gathered_place(row_quarter ^ quarter, column_order)
    link_own = tiles[:, own_rows - pad, :share].astype(jnp.int32)[place].reshape(-1)
    offset_own = (
        place[:, None] * share_rows + jnp.arange(share, dtype=jnp.int32)[None, :] * 2 * block
    ).reshape(-1)
    next_index = jnp.arange(half, dtype=jnp.int32)
    source = quarters // 2 + next_index // share
    inside = next_index % share
    holder = jnp.where(inside < part, source, source - quarters // 2)
    holder_place = gathered_place(holder ^ quarter, column_order)
    inside = inside % part
    link_next = tiles[:, share_rows - pad, :part].astype(jnp.int32)[holder_place, inside]
    offset_next = holder_place * share_rows + own_rows + inside * 2 * block

    def picked(mine, theirs, link):
        same = mine[:, :, None] == theirs[link][:, None, :]
        column = jnp.sum(
            jnp.where(same, jnp.arange(per_quarter, dtype=jnp.int32)[None, None, :], 0), axis=2
        )
        return jnp.where(jnp.any(same, axis=2), link[:, None] * per_quarter + column, count)

    pick_own = picked(codes, codes_near, link_own)
    pick_next = picked(codes_near, codes_far, link_next)
    target_place = gathered_place(target_slab ^ slab, row_order) * here + target_local
    index = jnp.concatenate(
        [
            offset_own,
            offset_next,
            pick_own.reshape(-1),
            pick_next.reshape(-1),
            target_place.reshape(-1),
            even.astype(jnp.int32)[None],
        ]
    )

    steps = 4
    per_step = rows // steps
    anywhere = pl.BlockSpec(memory_space=pl.ANY)
    whole = pl.BlockSpec(memory_space=pltpu.VMEM)
    row_spec = pl.BlockSpec((per_step, per_quarter, block, block), lambda s, _: (s, 0, 0, 0))
    scratch = pltpu.VMEM(((count + 1) * block, block), jnp.bfloat16)
    kernel = functools.partial(
        sweep_kernel, chunks, rows, per_quarter, block, half, per_step, own_rows, share_rows, next_rows
    )
    return pl.pallas_call(
        kernel,
        grid_spec=pltpu.PrefetchScalarGridSpec(
            num_scalar_prefetch=1,
            grid=(steps,),
            in_specs=[row_spec] + [anywhere] * (3 * chunks) + [whole, whole],
            out_specs=row_spec,
            scratch_shapes=[scratch, scratch, scratch, pltpu.SemaphoreType.DMA((2, chunks))],
        ),
        out_shape=jax.ShapeDtypeStruct(prior.shape, prior.dtype),
        compiler_params=pltpu.CompilerParams(
            vmem_limit_bytes=48 * 1024 * 1024, dimension_semantics=("arbitrary",)
        ),
        cost_estimate=pl.CostEstimate(flops=3 * 10**9, bytes_accessed=8 * 2**20, transcendentals=0),
    )(index, prior, *near, *passed, *far, weights, targets)


def solution(mesh):
    placed = (
        P("rows", "cols", None, None),
        P("rows", "cols"),
        P(("rows", "cols")),
        P(("rows", "cols"), None, None, None),
        P(("rows", "cols"), None, None),
    )
    return jax.shard_map(
        local, mesh=mesh, in_specs=placed, out_specs=P("rows", "cols", None, None), check_vma=False
    )
```

time: 300 us -> 113 us (0.38)
  the two profiles are of different devices: /device:TPU:10 before, /device:TPU:28 now
where the time goes in v1:
time: 113 us
  waiting for transfers between devices  58.9 us (52%)
  starting transfers between devices  19.5 us (17%)
  Pallas kernels  14.6 us (13%)
  local copies, waits for them, and re-layouts  10.5 us (9%)
  other arithmetic  9.13 us (8%)
    ppermute x5, waiting for transfers between devices, exchange(): return lax.ppermute(array, axis, [(i, i ^ mask) for i in range(count)])  37.7 us
    ppermute x2, waiting for transfers between devices, local(): passed = [lax.ppermute(x, 'rows', to_odd) for x in far]  20.4 us
    pallas_call x1, Pallas kernels, local(): pl.pallas_call(kernel, grid_spec=pltpu.PrefetchScalarGridSpec(num_scalar_...  12.9 us
    ppermute x5, starting transfers between devices, exchange(): return lax.ppermute(array, axis, [(i, i ^ mask) for i in range(count)])  8.25 us
    ppermute x2, starting transfers between devices, local(): near = [lax.ppermute(x, 'rows', to_even) for x in sent]  5.64 us
    concatenate x3, other arithmetic, local(): jnp.concatenate([targets, exchange(targets, 'rows', mask)], axis=0)  3.02 us
    unnamed x19, local copies, waits for them, and re-layouts  2.89 us
    ppermute x2, starting transfers between devices, local(): passed = [lax.ppermute(x, 'rows', to_odd) for x in far]  2.57 us
  transfers between devices with their start and end apart: 13, of which 5 were waited for; matrix products, arithmetic and copies ran while one was open for 12% of the time, Pallas kernels for 1%

profile of v1, /device:TPU:28, one launch (start us, length us, event | category | flops | bytes accessed | tf_op | source)
XLA Modules:
  0.0 112.9 jit_solution(17319926707105392053)
XLA Ops:
  0.0 0.7 multiply_add_fusion
  0.8 0.1 copy.18
  0.9 0.1 concatenate.52
  1.1 0.1 copy.19
  1.2 0.1 concatenate.53
  1.3 2.1 %fusion.41 = (bf16[4,4,128,128]{3,2,1,0:T(8,128)(2,1)}, bf16[4,4,128,128]{3,2,1,0:T(8,128)(2,1)S(1)}) fusion(bf16[16,4,128,128]{3,2,1,0:T(8,128)(2,1)} %p_own.1), kind=kLoop, calls=%fused_computation.128 | loop fusion | bytes 2097152 | tf_op jit(solution)/shard_map/slice | solution.py:154
  3.5 0.8 pad_maximum_fusion.2
  4.3 0.4 collective-permute-start.1
  4.7 2.4 %collective-permute-start = (bf16[2064,128]{1,0:T(8,128)(2,1)}, bf16[2064,128]{1,0:T(8,128)(2,1)S(1)}, u32[]{:S(2)}, u32[]{:S(2)}) collective-permute-start(bf16[2064,128]{1,0:T(8,128)(2,1)} %pad_maximum_fusion.2), channel_id=1, source_target_pairs={{4,0},{12,8},{20,16},{28,24},{5,1},{13,9},{21,17},{29,25},{6,2},{1... | collective-permute-start | bytes 1585160 | tf_op jit(solution)/shard_map/ppermute | solution.py:170
  7.3 0.7 fusion.2
  8.0 1.3 %collective-permute-start.3 = (bf16[528,128]{1,0:T(8,128)(2,1)}, bf16[528,128]{1,0:T(8,128)(2,1)}, u32[]{:S(2)}, u32[]{:S(2)}) collective-permute-start(bf16[528,128]{1,0:T(8,128)(2,1)} %fusion.2), channel_id=1, source_target_pairs={{6,2},{7,3},{10,6},{11,7},{14,10},{15,11},{18,14},{19,15},{22,18},... | collective-permute-start | bytes 405512 | tf_op jit(solution)/shard_map/ppermute | solution.py:183
  9.3 0.7 fusion.3
  9.9 1.3 %collective-permute-start.4 = (bf16[528,128]{1,0:T(8,128)(2,1)}, bf16[528,128]{1,0:T(8,128)(2,1)S(1)}, u32[]{:S(2)}, u32[]{:S(2)}) collective-permute-start(bf16[528,128]{1,0:T(8,128)(2,1)} %fusion.3), channel_id=1, source_target_pairs={{6,0},{7,1},{10,4},{11,5},{14,8},{15,9},{18,12},{19,13},{22,16},{2... | collective-permute-start | bytes 405512 | tf_op jit(solution)/shard_map/ppermute | solution.py:184
  11.2 1.6 %shard_map.55 = bf16[4,128,128]{2,1,0:T(8,128)(2,1)} custom-call(bf16[4,128,128]{2,1,0:T(8,128)(2,1)} %src.1), custom_call_target="tpu_custom_call" | custom-call | tf_op jit(solution)/shard_map/pallas_call | solution.py:193
  12.9 0.4 collective-permute-start.10
  13.7 0.1 reshape.373
  13.8 9.1 %collective-permute-done.10 = bf16[4,128,128]{2,1,0:T(8,128)(2,1)S(1)} collective-permute-done((bf16[4,128,128]{2,1,0:T(8,128)(2,1)}, bf16[4,128,128]{2,1,0:T(8,128)(2,1)S(1)}, u32[]{:S(2)}, u32[]{:S(2)}) %collective-permute-start.10) | collective-permute-done | bytes 131104 | tf_op jit(solution)/shard_map/ppermute | solution.py:21
  22.9 0.9 pad_maximum_fusion.5
  23.8 3.2 %collective-permute-start.7 = (bf16[2048,128]{1,0:T(8,128)(2,1)}, bf16[2048,128]{1,0:T(8,128)(2,1)}, u32[]{:S(2)}, u32[]{:S(2)}) collective-permute-start(bf16[2048,128]{1,0:T(8,128)(2,1)} %bitcast.40), channel_id=1, source_target_pairs={{4,0},{12,8},{20,16},{28,24},{5,1},{13,9},{21,17},{29,25},{6,2},{1... | collective-permute-start | bytes 1572872 | tf_op jit(solution)/shard_map/ppermute | solution.py:170
  27.0 0.8 collective-permute-done.4
  27.9 0.6 copy-done.6
  28.5 1.0 constant_dynamic-update-slice_fusion.2
  29.5 20.4 %collective-permute-done.11 = bf16[8,128,128]{2,1,0:T(8,128)(2,1)S(1)} collective-permute-done((bf16[8,128,128]{2,1,0:T(8,128)(2,1)S(1)}, bf16[8,128,128]{2,1,0:T(8,128)(2,1)S(1)}, u32[]{:S(2)}, u32[]{:S(2)}) %collective-permute-start.11) | collective-permute-done | bytes 262176 | tf_op jit(solution)/shard_map/ppermute | solution.py:21
  49.9 1.6 %collective-permute-start.5 = (bf16[1568,128]{1,0:T(8,128)(2,1)S(1)}, bf16[1568,128]{1,0:T(8,128)(2,1)S(1)}, u32[]{:S(2)}, u32[]{:S(2)}) collective-permute-start(bf16[1568,128]{1,0:T(8,128)(2,1)S(1)} %pad_maximum_fusion.4), channel_id=1, source_target_pairs={{0,2},{1,3},{2,0},{3,1},{4,6},{5,7},{6,4},{7,5},{8,10},{9,11},{10,... | collective-permute-start | bytes 1204232 | tf_op jit(solution)/shard_map/ppermute | solution.py:21
  51.5 0.9 pad_maximum_fusion.3
  52.4 6.2 %collective-permute-start.12 = (bf16[16,128,128]{2,1,0:T(8,128)(2,1)}, bf16[16,128,128]{2,1,0:T(8,128)(2,1)}, u32[]{:S(2)}, u32[]{:S(2)}) collective-permute-start(bf16[16,128,128]{2,1,0:T(8,128)(2,1)} %pad_maximum_fusion.3), channel_id=1, source_target_pairs={{0,4},{4,0},{8,12},{12,8},{16,20},{20,16},{24,28},{28,24},{1,5},{5... | collective-permute-start | bytes 1572872 | tf_op jit(solution)/shard_map/ppermute | solution.py:21
  58.6 1.3 %collective-permute-start.9 = (bf16[2048,128]{1,0:T(8,128)(2,1)}, bf16[2048,128]{1,0:T(8,128)(2,1)}, u32[]{:S(2)}, u32[]{:S(2)}) collective-permute-start(bf16[2048,128]{1,0:T(8,128)(2,1)} %collective-permute-done.8.refs_5_), channel_id=1, source_target_pairs={{0,4},{8,12},{16,20},{24,28},{1,5},{9,13},{17,21},{25,29},{2,6},{1... | collective-permute-start | bytes 1572872 | tf_op jit(solution)/shard_map/ppermute | solution.py:171
  59.9 1.3 %collective-permute-start.2 = (bf16[2064,128]{1,0:T(8,128)(2,1)S(1)}, bf16[2064,128]{1,0:T(8,128)(2,1)}, u32[]{:S(2)}, u32[]{:S(2)}) collective-permute-start(bf16[2064,128]{1,0:T(8,128)(2,1)S(1)} %collective-permute-done.1.refs_4_), channel_id=1, source_target_pairs={{0,4},{8,12},{16,20},{24,28},{1,5},{9,13},{17,21},{25,29},{2,6},{1... | collective-permute-start | bytes 1585160 | tf_op jit(solution)/shard_map/ppermute | solution.py:171
  61.3 1.0 pad_maximum_fusion.1
  62.3 0.1 add_reduce_fusion
  62.5 1.1 constant_dynamic-update-slice_fusion.1
  63.5 8.2 %collective-permute-done.12 = bf16[16,128,128]{2,1,0:T(8,128)(2,1)} collective-permute-done((bf16[16,128,128]{2,1,0:T(8,128)(2,1)}, bf16[16,128,128]{2,1,0:T(8,128)(2,1)}, u32[]{:S(2)}, u32[]{:S(2)}) %collective-permute-start.12) | collective-permute-done | bytes 524320 | tf_op jit(solution)/shard_map/ppermute | solution.py:21
  71.7 1.2 %pad_maximum_fusion.refs_7_ = bf16[32,128,128]{2,1,0:T(8,128)(2,1)S(1)} fusion(bf16[16,128,128]{2,1,0:T(8,128)(2,1)} %collective-permute-done.12, bf16[8,128,128]{2,1,0:T(8,128)(2,1)} %copy-done.5, bf16[4,128,128]{2,1,0:T(8,128)(2,1)S(1)} %collective-permute-done.10, bf16[4,128,128]{2,1,0:T(8,128)(2,1)S(1)} %copy-done.3), kind=kLoop, calls=%fused_computation.4 | loop fusion | flops 1572864 | bytes 2097152 | tf_op jit(solution)/shard_map/concatenate | solution.py:198
  72.9 20.4 %collective-permute-done.2.refs_2_ = bf16[2064,128]{1,0:T(8,128)(2,1)} collective-permute-done((bf16[2064,128]{1,0:T(8,128)(2,1)S(1)}, bf16[2064,128]{1,0:T(8,128)(2,1)}, u32[]{:S(2)}, u32[]{:S(2)}) %collective-permute-start.2) | collective-permute-done | bytes 528416 | tf_op jit(solution)/shard_map/ppermute | solution.py:171
  93.3 0.7 slice_convert_fusion.1
  94.0 0.1 fusion.15
  94.2 0.1 copy.23
  94.2 1.2 %constant_dynamic-update-slice_fusion.refs_6_ = bf16[6272,128]{1,0:T(8,128)(2,1)S(1)} fusion(bf16[6272,128]{1,0:T(8,128)(2,1)S(1)} %constant_dynamic-update-slice_fusion.1, bf16[3136,128]{1,0:T(8,128)(2,1)} %collective-permute-done.6), kind=kLoop, calls=%fused_computation.16 | loop fusion | bytes 1605632 | tf_op jit(solution)/shard_map/concatenate | solution.py:191
  95.5 0.6 gather_fusion
  96.1 0.1 reshape.372
  96.2 0.1 copy.29
  96.3 0.7 gather_fusion.2
  97.0 0.6 gather_fusion.3
  97.9 0.6 gather_fusion.1
  98.7 0.1 select_n.268
  98.8 0.1 concatenate.62.index
  98.9 1.0 copy-done.1
  100.0 12.9 %shard_map.56 = bf16[16,4,128,128]{3,2,1,0:T(8,128)(2,1)} custom-call(s32[185]{0:T(256)S(1)} %concatenate.62.index, bf16[16,4,128,128]{3,2,1,0:T(8,128)(2,1)} %p_own.1, bf16[2064,128]{1,0:T(8,128)(2,1)S(1)} %copy-done.1, bf16[2048,128]{1,0:T(8,128)(2,1)} %collective-permute-done.7.refs_1_, bf16[2064,128]{1,0:T(8,128)(2,1)} %collective-permute-done.2.refs_2_, ...), custom_call_target="tpu_custom_call" | custom-call | flops 3000000000 | bytes 8388608 | tf_op jit(solution)/shard_map/pallas_call | solution.py:253
  (68 shorter events, 1.6 us)
Async XLA Ops:
  0.0 7.2 %copy-start.2 = (bf16[4,2,128,128]{3,2,1,0:T(8,128)(2,1)S(1)}, bf16[4,2,128,128]{3,2,1,0:T(8,128)(2,1)}, u32[]{:S(2)}) copy-start(bf16[4,2,128,128]{3,2,1,0:T(8,128)(2,1)} %param.8) | copy-start | bytes 786436
  1.3 5.9 %copy-start.7 = (s32[4]{0:T(128)S(1)}, s32[4]{0:T(128)}, u32[]{:S(2)}) copy-start(s32[4]{0:T(128)} %param.7) | copy-start | bytes 52
  4.3 54.3 %collective-permute-start.1 = (bf16[2064,128]{1,0:T(8,128)(2,1)}, bf16[2064,128]{1,0:T(8,128)(2,1)S(1)}, u32[]{:S(2)}, u32[]{:S(2)}) collective-permute-start(bf16[2064,128]{1,0:T(8,128)(2,1)} %pad_maximum_fusion.2), channel_id=1, source_target_pairs={{0,24},{4,28},{8,0},{12,4},{16,8},{20,12},{24,16},{28,20},{1,25},{... | collective-permute-start | bytes 1585160 | tf_op jit(solution)/shard_map/ppermute | solution.py:169
  4.7 55.2 %collective-permute-start = (bf16[2064,128]{1,0:T(8,128)(2,1)}, bf16[2064,128]{1,0:T(8,128)(2,1)S(1)}, u32[]{:S(2)}, u32[]{:S(2)}) collective-permute-start(bf16[2064,128]{1,0:T(8,128)(2,1)} %pad_maximum_fusion.2), channel_id=1, source_target_pairs={{4,0},{12,8},{20,16},{28,24},{5,1},{13,9},{21,17},{29,25},{6,2},{1... | collective-permute-start | bytes 1585160 | tf_op jit(solution)/shard_map/ppermute | solution.py:170
  8.0 15.8 %collective-permute-start.3 = (bf16[528,128]{1,0:T(8,128)(2,1)}, bf16[528,128]{1,0:T(8,128)(2,1)}, u32[]{:S(2)}, u32[]{:S(2)}) collective-permute-start(bf16[528,128]{1,0:T(8,128)(2,1)} %fusion.2), channel_id=1, source_target_pairs={{6,2},{7,3},{10,6},{11,7},{14,10},{15,11},{18,14},{19,15},{22,18},... | collective-permute-start | bytes 405512 | tf_op jit(solution)/shard_map/ppermute | solution.py:183
  9.9 17.9 %collective-permute-start.4 = (bf16[528,128]{1,0:T(8,128)(2,1)}, bf16[528,128]{1,0:T(8,128)(2,1)S(1)}, u32[]{:S(2)}, u32[]{:S(2)}) collective-permute-start(bf16[528,128]{1,0:T(8,128)(2,1)} %fusion.3), channel_id=1, source_target_pairs={{6,0},{7,1},{10,4},{11,5},{14,8},{15,9},{18,12},{19,13},{22,16},{2... | collective-permute-start | bytes 405512 | tf_op jit(solution)/shard_map/ppermute | solution.py:184
  12.9 38.7 %copy-start.3 = (bf16[4,128,128]{2,1,0:T(8,128)(2,1)S(1)}, bf16[4,128,128]{2,1,0:T(8,128)(2,1)}, u32[]{:S(2)}) copy-start(bf16[4,128,128]{2,1,0:T(8,128)(2,1)} %shard_map.55) | copy-start | bytes 393220
  12.9 10.0 %collective-permute-start.10 = (bf16[4,128,128]{2,1,0:T(8,128)(2,1)}, bf16[4,128,128]{2,1,0:T(8,128)(2,1)S(1)}, u32[]{:S(2)}, u32[]{:S(2)}) collective-permute-start(bf16[4,128,128]{2,1,0:T(8,128)(2,1)} %shard_map.55), channel_id=1, source_target_pairs={{0,8},{4,12},{8,0},{12,4},{16,24},{20,28},{24,16},{28,20},{1,9},{5... | collective-permute-start | bytes 393224 | tf_op jit(solution)/shard_map/ppermute | solution.py:21
  22.9 29.6 %collective-permute-start.8 = (bf16[2048,128]{1,0:T(8,128)(2,1)}, bf16[2048,128]{1,0:T(8,128)(2,1)}, u32[]{:S(2)}, u32[]{:S(2)}) collective-permute-start(bf16[2048,128]{1,0:T(8,128)(2,1)} %bitcast.39), channel_id=1, source_target_pairs={{0,24},{4,28},{8,0},{12,4},{16,8},{20,12},{24,16},{28,20},{1,25},{... | collective-permute-start | bytes 1572872 | tf_op jit(solution)/shard_map/ppermute | solution.py:169
  23.8 75.1 %collective-permute-start.7 = (bf16[2048,128]{1,0:T(8,128)(2,1)}, bf16[2048,128]{1,0:T(8,128)(2,1)}, u32[]{:S(2)}, u32[]{:S(2)}) collective-permute-start(bf16[2048,128]{1,0:T(8,128)(2,1)} %bitcast.40), channel_id=1, source_target_pairs={{4,0},{12,8},{20,16},{28,24},{5,1},{13,9},{21,17},{29,25},{6,2},{1... | collective-permute-start | bytes 1572872 | tf_op jit(solution)/shard_map/ppermute | solution.py:170
  27.9 0.6 copy-start.6
  27.9 22.1 %collective-permute-start.11 = (bf16[8,128,128]{2,1,0:T(8,128)(2,1)S(1)}, bf16[8,128,128]{2,1,0:T(8,128)(2,1)S(1)}, u32[]{:S(2)}, u32[]{:S(2)}) collective-permute-start(bf16[8,128,128]{2,1,0:T(8,128)(2,1)S(1)} %pad_maximum_fusion.5), channel_id=1, source_target_pairs={{0,16},{4,20},{8,24},{12,28},{16,0},{20,4},{24,8},{28,12},{1,17},{... | collective-permute-start | bytes 786440 | tf_op jit(solution)/shard_map/ppermute | solution.py:21
  49.9 11.3 %copy-start.5 = (bf16[8,128,128]{2,1,0:T(8,128)(2,1)}, bf16[8,128,128]{2,1,0:T(8,128)(2,1)S(1)}, u32[]{:S(2)}) copy-start(bf16[8,128,128]{2,1,0:T(8,128)(2,1)S(1)} %collective-permute-done.11) | copy-start | bytes 786436
  49.9 11.3 %collective-permute-start.5 = (bf16[1568,128]{1,0:T(8,128)(2,1)S(1)}, bf16[1568,128]{1,0:T(8,128)(2,1)S(1)}, u32[]{:S(2)}, u32[]{:S(2)}) collective-permute-start(bf16[1568,128]{1,0:T(8,128)(2,1)S(1)} %pad_maximum_fusion.4), channel_id=1, source_target_pairs={{0,2},{1,3},{2,0},{3,1},{4,6},{5,7},{6,4},{7,5},{8,10},{9,11},{10,... | collective-permute-start | bytes 1204232 | tf_op jit(solution)/shard_map/ppermute | solution.py:21
  52.4 19.3 %collective-permute-start.12 = (bf16[16,128,128]{2,1,0:T(8,128)(2,1)}, bf16[16,128,128]{2,1,0:T(8,128)(2,1)}, u32[]{:S(2)}, u32[]{:S(2)}) collective-permute-start(bf16[16,128,128]{2,1,0:T(8,128)(2,1)} %pad_maximum_fusion.3), channel_id=1, source_target_pairs={{0,4},{4,0},{8,12},{12,8},{16,20},{20,16},{24,28},{28,24},{1,5},{5... | collective-permute-start | bytes 1572872 | tf_op jit(solution)/shard_map/ppermute | solution.py:21
  58.6 40.3 %collective-permute-start.9 = (bf16[2048,128]{1,0:T(8,128)(2,1)}, bf16[2048,128]{1,0:T(8,128)(2,1)}, u32[]{:S(2)}, u32[]{:S(2)}) collective-permute-start(bf16[2048,128]{1,0:T(8,128)(2,1)} %collective-permute-done.8.refs_5_), channel_id=1, source_target_pairs={{0,4},{8,12},{16,20},{24,28},{1,5},{9,13},{17,21},{25,29},{2,6},{1... | collective-permute-start | bytes 1572872 | tf_op jit(solution)/shard_map/ppermute | solution.py:171
  59.9 3.6 %copy-start = (bf16[2064,128]{1,0:T(8,128)(2,1)}, bf16[2064,128]{1,0:T(8,128)(2,1)S(1)}, u32[]{:S(2)}) copy-start(bf16[2064,128]{1,0:T(8,128)(2,1)S(1)} %collective-permute-done.refs_0_) | copy-start | bytes 1585156
  59.9 33.4 %collective-permute-start.2 = (bf16[2064,128]{1,0:T(8,128)(2,1)S(1)}, bf16[2064,128]{1,0:T(8,128)(2,1)}, u32[]{:S(2)}, u32[]{:S(2)}) collective-permute-start(bf16[2064,128]{1,0:T(8,128)(2,1)S(1)} %collective-permute-done.1.refs_4_), channel_id=1, source_target_pairs={{0,4},{8,12},{16,20},{24,28},{1,5},{9,13},{17,21},{25,29},{2,6},{1... | collective-permute-start | bytes 1585160 | tf_op jit(solution)/shard_map/ppermute | solution.py:171
  61.3 1.0 copy-start.4
  62.3 31.9 %collective-permute-start.6 = (bf16[3136,128]{1,0:T(8,128)(2,1)}, bf16[3136,128]{1,0:T(8,128)(2,1)}, u32[]{:S(2)}, u32[]{:S(2)}) collective-permute-start(bf16[3136,128]{1,0:T(8,128)(2,1)} %pad_maximum_fusion.1), channel_id=1, source_target_pairs={{0,1},{1,0},{2,3},{3,2},{4,5},{5,4},{6,7},{7,6},{8,9},{9,8},{10,11... | collective-permute-start | bytes 2408456 | tf_op jit(solution)/shard_map/ppermute | solution.py:21
  98.9 1.0 copy-start.1

commit v2 on v0

v2 whole, which is shorter than its diff:
```python
import functools

import jax
import jax.numpy as jnp
from jax import lax
from jax.experimental import pallas as pl
from jax.experimental.pallas import tpu as pltpu
from jax.sharding import PartitionSpec as P

mixing = 0.75
pad = 16
plan = {'sizes': (4, 4),
 'gates': {'Y1': ['Y0'], 'T': ['I1'], 'I1': ['Z0'], 'I2': ['Z0']},
 'order': ['Z0', 'I', 'Z1', 'T', 'KM', 'Y0', 'X', 'Y1', 'E1', 'E2', 'E3'],
 'cost': 0,
 'groups': 4,
 'vmem': 48,
 'any': True}


def bits_of(count):
    return count.bit_length() - 1


def exchange(array, axis, mask):
    count = lax.axis_size(axis)
    return lax.ppermute(array, axis, [(i, i ^ mask) for i in range(count)])


def taken_from(array, axis, ahead):
    count = lax.axis_size(axis)
    return lax.ppermute(array, axis, [(i, (i - ahead) % count) for i in range(count)])


def after(array, *others):
    return lax.optimization_barrier((array, *others))[0] if others else array


def gathered_place(distance, order):
    place = jnp.zeros_like(distance)
    for step, mask in enumerate(order):
        place = place + jnp.where((distance & mask) != 0, 1 << step, 0)
    return place


def transpose_kernel(src, dst):
    for t in range(src.shape[0]):
        dst[t] = src[t].T


def tile_of(values):
    return jnp.pad(values.astype(jnp.bfloat16)[None, :], ((0, pad - 1), (0, 128 - values.shape[0])))


def row_slice(ref, start, size):
    return ref[pl.ds(pl.multiple_of(start, pad), size), :]


def side(blocks):
    return jnp.concatenate(blocks, axis=1)


def assemble(pieces, sems):
    copies = [
        pltpu.make_async_copy(
            source.at[pl.ds(at, size), :], target.at[pl.ds(to, size), :], sems.at[n]
        )
        for n, (source, at, size, target, to) in enumerate(pieces)
    ]
    for copy in copies:
        copy.start()
    return copies


def left_kernel(layout, rows, per_quarter, block, half, index, prior, *refs):
    first, second, p1, p2, weights, first_next, sems = refs[-7:]
    targets = (p1, p2, weights)
    count = half * per_quarter
    copies = assemble(
        [(refs[n], at, size, targets[which], to) for n, at, size, which, to in layout], sems
    )
    at_next = rows
    at_pick = at_next + half
    at_pick_next = at_pick + rows * per_quarter

    def row_weights(offset):
        return side([row_slice(weights, offset, block), row_slice(weights, offset + block, block)])

    def blk(ref, n):
        return ref[pl.ds(pl.multiple_of(n * block, block), block), :]

    zero = jnp.zeros((block, block), jnp.bfloat16)
    for ref in (p1, p2, first_next):
        ref[pl.ds(count * block, block), :] = zero
    for copy in copies:
        copy.wait()
    for j in range(half):
        top = side([blk(p1, j * per_quarter + k) for k in range(per_quarter)])
        low = side([blk(p2, index[at_pick_next + j * per_quarter + k]) for k in range(per_quarter)])
        got = jnp.dot(
            row_weights(index[at_next + j]),
            jnp.concatenate([top, low], axis=0),
            preferred_element_type=jnp.float32,
        ).astype(jnp.bfloat16)
        for k in range(per_quarter):
            first_next[pl.ds((j * per_quarter + k) * block, block), :] = got[:, k * block : (k + 1) * block]
    for i in range(rows):
        own = side([prior[i, k] for k in range(per_quarter)])
        cross = side([blk(p1, index[at_pick + i * per_quarter + k]) for k in range(per_quarter)])
        first[i] = jnp.dot(
            row_weights(index[i]),
            jnp.concatenate([own, cross], axis=0),
            preferred_element_type=jnp.float32,
        ).astype(jnp.bfloat16)
    for i in range(rows):
        cross = side([blk(first_next, index[at_pick + i * per_quarter + k]) for k in range(per_quarter)])
        second[i] = jnp.dot(
            row_weights(index[i]),
            jnp.concatenate([first[i], cross], axis=0),
            preferred_element_type=jnp.float32,
        ).astype(jnp.bfloat16)


def right_kernel(layout, rows, per_quarter, block, groups, index, prior, first, second, *refs):
    out, targets, swept, result, sems, out_sems = refs[-6:]
    copies = assemble([(refs[n], at, size, targets, to) for n, at, size, to in layout], sems)
    for copy in copies:
        copy.wait()

    def target(i, k):
        return targets[pl.ds(pl.multiple_of(index[i * per_quarter + k] * block, block), block), :]

    def cut(k):
        return slice(k * block, (k + 1) * block)

    per_group = rows // groups
    sent = []
    for g in range(groups):
        mine = range(g * per_group, (g + 1) * per_group)
        for i in mine:
            for k in range(per_quarter):
                image = jnp.dot(second[i, :, cut(k)], target(i, k), preferred_element_type=jnp.float32)
                swept[i, :, cut(k)] = (
                    mixing * image + (1.0 - mixing) * first[i, :, cut(k)].astype(jnp.float32)
                ).astype(jnp.bfloat16)
        for i in mine:
            for k in range(per_quarter):
                last = jnp.dot(swept[i, :, cut(k)], target(i, k), preferred_element_type=jnp.float32)
                result[i, k] = (
                    mixing * last + (1.0 - mixing) * prior[i, k].astype(jnp.float32)
                ).astype(jnp.bfloat16)
        span = pl.ds(g * per_group, per_group)
        copy = pltpu.make_async_copy(result.at[span], out.at[span], out_sems.at[g])
        copy.start()
        sent.append(copy)
    for copy in sent:
        copy.wait()


def local(prior, candidates, cross_link, a1_blocks, a2_blocks):
    rows, per_quarter, block = prior.shape[:3]
    here = a2_blocks.shape[0]
    slabs = lax.axis_size("rows")
    quarters = lax.axis_size("cols")
    slab = lax.axis_index("rows")
    quarter = lax.axis_index("cols")
    half = rows // 2
    share = a1_blocks.shape[0]
    part = share // 2
    count = half * per_quarter
    sizes = plan["sizes"]
    chunks = len(sizes)
    starts = [sum(sizes[:c]) for c in range(chunks)]
    even = slab % 2 == 0
    there = {}

    def gated(array, name):
        return after(array, *[there[n] for n in plan["gates"].get(name, ())])

    def record(name, array):
        there[name] = array
        return array

    target_slab = candidates >> bits_of(quarters * here)
    target_local = candidates & (here - 1)
    t_rows = here * block
    anywhere = pl.BlockSpec(memory_space=pl.ANY)
    whole = pl.BlockSpec(memory_space=pltpu.VMEM)
    scalars = pl.BlockSpec(memory_space=pltpu.SMEM)

    mine = [
        prior[half + starts[c] : half + starts[c] + sizes[c]].reshape(-1, block) for c in range(chunks)
    ]
    links = cross_link % rows - half
    own_weights = jnp.concatenate([a1_blocks.reshape(-1, block), tile_of(links)], axis=0)
    parts = [
        jnp.concatenate(
            [a1_blocks[c * part : (c + 1) * part].reshape(-1, block), tile_of(links[c * part : (c + 1) * part])],
            axis=0,
        )
        for c in range(2)
    ]
    turned = pl.pallas_call(
        transpose_kernel, out_shape=jax.ShapeDtypeStruct(a2_blocks.shape, a2_blocks.dtype)
    )(a2_blocks).reshape(-1, block)

    far, near = {}, {}
    column = {}

    def do_far(c):
        payload = mine[c]
        got = taken_from(gated(payload, "Z%d" % c), "rows", 2)
        far[c] = record("Z%d" % c, got)

    def do_near(c):
        payload = jnp.where(even, far[c], mine[c])
        near[c] = record("Y%d" % c, exchange(gated(payload, "Y%d" % c), "rows", 1))

    def do_pair():
        got = record("T", exchange(gated(turned, "T"), "rows", 1))
        column[0] = jnp.concatenate([turned, got], axis=0)

    def do_column(d):
        column[d] = record("E%d" % d, taken_from(gated(column[0], "E%d" % d), "rows", 2 * d))

    both = ("rows", "cols")
    upper = range(quarters // 2, quarters)
    kept = [(((s + 1) % slabs) * quarters + q, s * quarters + q) for s in range(slabs) for q in upper]
    moved = [
        (((s + 1) % slabs) * quarters + q, s * quarters + q - quarters // 2)
        for s in range(slabs)
        for q in upper
    ]
    column_order = [1 << b for b in reversed(range(bits_of(quarters)))]
    w = {}

    def do_next():
        w["kept"] = record("K", lax.ppermute(gated(parts[0], "K"), both, kept))
        w["moved"] = record("M", lax.ppermute(gated(parts[1], "M"), both, moved))

    def do_columns():
        next_part = jnp.where(quarter >= quarters // 2, w["kept"], w["moved"])
        base = jnp.concatenate([own_weights, next_part], axis=0)
        w["pieces"] = [base]
        for n, mask in enumerate(column_order):
            got = record("X%d" % n, exchange(gated(base, "X%d" % n), "cols", mask))
            w["pieces"].append(got)
            base = jnp.concatenate([base, got], axis=0)
        w["all"] = base

    few = slabs == 8
    if few:
        distances = range(1, slabs // 2)
    else:
        distances = ()

    def do_ids():
        for ahead in (1, 2):
            record("I%d" % ahead, taken_from(gated(candidates[half:], "I%d" % ahead), "rows", ahead))

    for name in plan["order"]:
        if name[0] == "Z":
            do_far(int(name[1:]))
        elif name[0] == "Y":
            do_near(int(name[1:]))
        elif name == "I":
            do_ids()
        elif name == "KM":
            do_next()
        elif name == "X":
            do_columns()
        elif name[0] == "E" and few:
            do_column(int(name[1:]))
        elif name == "T" and few:
            do_pair()
    row_order = [1 << b for b in range(1, bits_of(slabs))]
    if not few:
        base = turned
        for mask in row_order:
            base = jnp.concatenate([base, exchange(base, "rows", mask)], axis=0)
        swapped = exchange(base, "rows", 1)

    own_rows = own_weights.shape[0]
    share_rows = own_rows + parts[0].shape[0]
    tiles = w["all"].reshape(quarters, share_rows, block)
    row_quarter = jnp.arange(quarters, dtype=jnp.int32)
    place = gathered_place(row_quarter ^ quarter, column_order)

    def taken(table, at):
        same = at[..., None] == jnp.arange(table.shape[0], dtype=jnp.int32)
        return jnp.sum(
            jnp.where(same.reshape(same.shape + (1,) * (table.ndim - 1)), table, 0), axis=at.ndim
        )

    link_own = taken(tiles[:, own_rows - pad, :share].astype(jnp.int32), place).reshape(-1)
    offset_own = (
        place[:, None] * share_rows + jnp.arange(share, dtype=jnp.int32)[None, :] * 2 * block
    ).reshape(-1)
    next_index = jnp.arange(half, dtype=jnp.int32)
    source = quarters // 2 + next_index // share
    inside = next_index % share
    holder = jnp.where(inside < part, source, source - quarters // 2)
    holder_place = gathered_place(holder ^ quarter, column_order)
    inside = inside % part
    link_next = taken(
        tiles[:, share_rows - pad, :part].astype(jnp.int32).reshape(-1), holder_place * part + inside
    )
    offset_next = holder_place * share_rows + own_rows + inside * 2 * block

    def picked(ours, theirs, link):
        same = ours[:, :, None] == taken(theirs, link)[:, None, :]
        which = jnp.sum(
            jnp.where(same, jnp.arange(per_quarter, dtype=jnp.int32)[None, None, :], 0), axis=2
        )
        return jnp.where(jnp.any(same, axis=2), link[:, None] * per_quarter + which, count)

    pick_own = picked(candidates, there["I1"], link_own)
    pick_next = picked(there["I1"], there["I2"], link_next)
    index = jnp.concatenate(
        [offset_own, offset_next, pick_own.reshape(-1), pick_next.reshape(-1)]
    )
    odd_one = (target_slab ^ slab) & 1
    base_slab = slab ^ odd_one
    if few:
        ahead = ((target_slab - base_slab) % slabs) // 2
    else:
        ahead = gathered_place(target_slab ^ base_slab, row_order)
    target_place = (odd_one * (slabs // 2) + ahead) * here + target_local
    t_index = target_place.reshape(-1)

    params = pltpu.CompilerParams(vmem_limit_bytes=plan["vmem"] * 1024 * 1024)

    plan_space = anywhere if plan["any"] else whole
    arrays, layout = [], []

    def piece(array, at, size, *where):
        for n, known in enumerate(arrays):
            if known is array:
                break
        else:
            n = len(arrays)
            arrays.append(array)
        layout.append((n, at, size, *where))

    for c in range(chunks):
        size = sizes[c] * per_quarter * block
        piece(near[c], 0, size, 0, starts[c] * per_quarter * block)
        piece(far[c], 0, size, 1, starts[c] * per_quarter * block)
    to = 0
    for array in w["pieces"]:
        piece(array, 0, array.shape[0], 2, to)
        to += array.shape[0]
    wide = jax.ShapeDtypeStruct((rows, block, per_quarter * block), jnp.bfloat16)
    stack = pltpu.VMEM(((count + 1) * block, block), jnp.bfloat16)
    first, second = pl.pallas_call(
        functools.partial(left_kernel, tuple(layout), rows, per_quarter, block, half),
        in_specs=[scalars, whole] + [plan_space] * len(arrays),
        out_specs=[whole, whole],
        out_shape=[wide, wide],
        scratch_shapes=[
            stack,
            stack,
            pltpu.VMEM((to, block), jnp.bfloat16),
            stack,
            pltpu.SemaphoreType.DMA((len(layout),)),
        ],
        compiler_params=params,
        cost_estimate=pl.CostEstimate(flops=plan["cost"] * 10**9, bytes_accessed=8 * 2**20, transcendentals=0),
    )(index, prior, *arrays)

    arrays, layout = [], []
    if few:
        for d in range(slabs // 2):
            piece(column[d], 0, t_rows, d * t_rows)
            piece(column[d], t_rows, t_rows, (slabs // 2 + d) * t_rows)
    else:
        piece(base, 0, base.shape[0], 0)
        piece(swapped, 0, base.shape[0], base.shape[0])
    groups = plan["groups"]
    return pl.pallas_call(
        functools.partial(right_kernel, tuple(layout), rows, per_quarter, block, groups),
        in_specs=[scalars, whole, whole, whole] + [plan_space] * len(arrays),
        out_specs=anywhere,
        out_shape=jax.ShapeDtypeStruct(prior.shape, prior.dtype),
        scratch_shapes=[
            pltpu.VMEM((slabs * t_rows, block), jnp.bfloat16),
            pltpu.VMEM(wide.shape, jnp.bfloat16),
            pltpu.VMEM(prior.shape, jnp.bfloat16),
            pltpu.SemaphoreType.DMA((len(layout),)),
            pltpu.SemaphoreType.DMA((groups,)),
        ],
        compiler_params=params,
        cost_estimate=pl.CostEstimate(flops=10**9, bytes_accessed=8 * 2**20, transcendentals=0),
    )(t_index, prior, first, second, *arrays)


def solution(mesh):
    placed = (
        P("rows", "cols", None, None),
        P("rows", "cols"),
        P(("rows", "cols")),
        P(("rows", "cols"), None, None, None),
        P(("rows", "cols"), None, None),
    )
    return jax.shard_map(
        local, mesh=mesh, in_specs=placed, out_specs=P("rows", "cols", None, None), check_vma=False
    )
```

time: 300 us -> 74.2 us (0.25)
  waiting for transfers between devices: 146 us -> 27.8 us
  local copies, waits for them, and re-layouts: 65.1 us -> 7.4 us
  starting transfers between devices: 43.2 us -> 19.8 us
  matrix products: 22.2 us -> 0 us
  between operations: 14.2 us -> 0.26 us
  Pallas kernels: 0 us -> 12.9 us
  blocking collectives: 4.27 us -> 0 us
  other arithmetic: 1.13 us -> 4.49 us
    all_to_all x4 -> x0, waiting for transfers between devices: 84.4 us -> none  [the longest x1 44.8 us: local(): lax.all_to_all(product, 'rows', split_axis=0, concat_axis=0, tiled=True)]
    all_to_all x4 -> x0, starting transfers between devices: 37.8 us -> none  [the longest x1 17.4 us: local(): lax.all_to_all(send_first, 'rows', split_axis=0, concat_axis=0, tiled=True)]
    ppermute x3 -> x14, waiting for transfers between devices: 61.4 us -> 27.8 us  [the longest x7 14.7 us: taken_from(): lax.ppermute(array, axis, [(i, (i - ahead) % count) for i in range(count)])]
    gather x12 -> x0, local copies, waits for them, and re-layouts: 23.7 us -> none  [the longest x6 14.1 us: left_product(): picked = jnp.take_along_axis(gathered, chosen[:, :, None, None], axis=1)]
    dot_general x5 -> x0, matrix products: 22.2 us -> none  [the longest x2 8.03 us: left_product(): jnp.einsum('ixy,ikyz->ikxz', cross_blocks, picked, preferred_element_type...]
    scatter x3 -> x0, local copies, waits for them, and re-layouts: 19.4 us -> none  [the longest x1 10.1 us: local(): send_first = empty.at[position].set(first.reshape(-1, block, block))]
    ppermute x3 -> x14, starting transfers between devices: 5.34 us -> 19.8 us  [the longest x7 15 us: taken_from(): lax.ppermute(array, axis, [(i, (i - ahead) % count) for i in range(count)])]
    pallas_call x0 -> x3, Pallas kernels: none -> 12.9 us  [the longest x1 5.78 us: local(): pl.pallas_call(functools.partial(left_kernel, tuple(layout), rows, per_qu...]
  transfers between devices with their start and end apart: 8 -> 14, of which waited for: 4 -> 5; matrix products, arithmetic and copies ran while one was open for 18% -> 12% of each run, Pallas kernels for 0% -> 10%
where the time goes in v2:
time: 74.2 us; the launch traced here: 72.7 us
  waiting for transfers between devices  27.8 us (37%)
  starting transfers between devices  19.8 us (27%)
  Pallas kernels  12.9 us (17%)
  local copies, waits for them, and re-layouts  7.4 us (10%)
  other arithmetic  4.49 us (6%)
    ppermute x7, starting transfers between devices, taken_from(): lax.ppermute(array, axis, [(i, (i - ahead) % count) for i in range(count)])  15 us
    ppermute x7, waiting for transfers between devices, taken_from(): lax.ppermute(array, axis, [(i, (i - ahead) % count) for i in range(count)])  14.7 us
    ppermute x5, waiting for transfers between devices, exchange(): return lax.ppermute(array, axis, [(i, i ^ mask) for i in range(count)])  13.1 us
    pallas_call x1, Pallas kernels, local(): pl.pallas_call(functools.partial(left_kernel, tuple(layout), rows, per_qu...  5.78 us
    pallas_call x1, Pallas kernels, local(): pl.pallas_call(functools.partial(right_kernel, tuple(layout), rows, per_q...  5.49 us
    ppermute x1, starting transfers between devices, do_next(): w['kept'] = record('K', lax.ppermute(gated(parts[0], 'K'), both, kept))  3.31 us
    slice x1, local copies, waits for them, and re-layouts, local(): prior[half + starts[c]:half + starts[c] + sizes[c]].reshape(-1, block)  2.09 us
    select_n x2, other arithmetic, do_near(): payload = jnp.where(even, far[c], mine[c])  1.99 us
  transfers between devices with their start and end apart: 14, of which 5 were waited for; matrix products, arithmetic and copies ran while one was open for 12% of the time, Pallas kernels for 10%

profile of v2, /device:TPU:10, one launch (start us, length us, event | category | flops | bytes accessed | tf_op | source)
XLA Modules:
  0.0 72.7 jit_solution(4758010236255587886)
XLA Ops:
  0.0 1.0 %fusion.21 = (bf16[2,2,128,128]{3,2,1,0:T(8,128)(2,1)S(1)}, bf16[2,2,128,128]{3,2,1,0:T(8,128)(2,1)S(1)}) fusion(bf16[4,2,128,128]{3,2,1,0:T(8,128)(2,1)} %param.8), kind=kLoop, calls=%fused_computation.84 | loop fusion | bytes 524288 | tf_op jit(solution)/shard_map/slice | solution.py:198
  1.1 0.7 fusion.17
  1.7 0.1 slice_bitcast_fusion
  1.8 3.3 %collective-permute-start = (bf16[528,128]{1,0:T(8,128)(2,1)S(1)}, bf16[528,128]{1,0:T(8,128)(2,1)S(1)}, u32[]{:S(2)}, u32[]{:S(2)}) collective-permute-start(bf16[528,128]{1,0:T(8,128)(2,1)S(1)} %fusion.2), channel_id=1, source_target_pairs={{6,2},{7,3},{10,6},{11,7},{14,10},{15,11},{18,14},{19,15},{22,18},... | collective-permute-start | bytes 405512 | tf_op jit(solution)/shard_map/ppermute | solution.py:238
  5.2 1.3 %collective-permute-start.1 = (bf16[528,128]{1,0:T(8,128)(2,1)S(1)}, bf16[528,128]{1,0:T(8,128)(2,1)S(1)}, u32[]{:S(2)}, u32[]{:S(2)}) collective-permute-start(bf16[528,128]{1,0:T(8,128)(2,1)S(1)} %fusion.3), channel_id=1, source_target_pairs={{6,0},{7,1},{10,4},{11,5},{14,8},{15,9},{18,12},{19,13},{22,16},{2... | collective-permute-start | bytes 405512 | tf_op jit(solution)/shard_map/ppermute | solution.py:239
  6.5 2.1 %fusion.20 = (bf16[4,4,128,128]{3,2,1,0:T(8,128)(2,1)}, bf16[4,4,128,128]{3,2,1,0:T(8,128)(2,1)S(1)}) fusion(bf16[16,4,128,128]{3,2,1,0:T(8,128)(2,1)} %prior.3), kind=kLoop, calls=%fused_computation.83 | loop fusion | bytes 2097152 | tf_op jit(solution)/shard_map/slice | solution.py:192
  8.5 3.6 %collective-permute-start.4 = (bf16[2048,128]{1,0:T(8,128)(2,1)S(1)}, bf16[2048,128]{1,0:T(8,128)(2,1)S(1)}, u32[]{:S(2)}, u32[]{:S(2)}) collective-permute-start(bf16[2048,128]{1,0:T(8,128)(2,1)S(1)} %bitcast.25), channel_id=1, source_target_pairs={{0,24},{4,28},{8,0},{12,4},{16,8},{20,12},{24,16},{28,20},{1,25},{... | collective-permute-start | bytes 1572872 | tf_op jit(solution)/shard_map/ppermute | solution.py:32
  12.2 0.4 collective-permute-start.8
  12.6 0.7 constant_dynamic-update-slice_fusion.4
  13.4 0.1 iota_compare_fusion.4
  13.4 0.6 fusion.22
  14.2 0.1 slice.35
  14.2 0.1 add.149
  14.3 1.6 %shard_map.56 = bf16[4,128,128]{2,1,0:T(8,128)(2,1)} custom-call(bf16[4,128,128]{2,1,0:T(8,128)(2,1)} %src.1), custom_call_target="tpu_custom_call" | custom-call | tf_op jit(solution)/shard_map/pallas_call | solution.py:203
  16.0 0.1 copy.20
  16.1 0.1 reshape.196.index
  16.2 0.7 constant_dynamic-update-slice_fusion.2
  16.9 0.1 collective-permute-start.2
  17.0 8.3 %collective-permute-done.4.refs_1_ = bf16[2048,128]{1,0:T(8,128)(2,1)S(1)} collective-permute-done((bf16[2048,128]{1,0:T(8,128)(2,1)S(1)}, bf16[2048,128]{1,0:T(8,128)(2,1)S(1)}, u32[]{:S(2)}, u32[]{:S(2)}) %collective-permute-start.4) | collective-permute-done | bytes 524320 | tf_op jit(solution)/shard_map/ppermute | solution.py:32
  25.3 4.0 %collective-permute-start.6 = (s32[8,4]{0,1:T(4,128)S(1)}, s32[8,4]{0,1:T(4,128)S(1)}, u32[]{:S(2)}, u32[]{:S(2)}) collective-permute-start(s32[8,4]{0,1:T(4,128)S(1)} %slice.35), channel_id=1, source_target_pairs={{0,24},{4,28},{8,0},{12,4},{16,8},{20,12},{24,16},{28,20},{1,25},{... | collective-permute-start | bytes 392 | tf_op jit(solution)/shard_map/ppermute | solution.py:32
  29.3 0.1 broadcast_select_fusion.1
  29.4 0.1 collective-permute-start.7
  29.6 0.1 collective-permute-start.3
  29.7 5.7 %collective-permute-done.8.refs_3_ = bf16[2048,128]{1,0:T(8,128)(2,1)S(1)} collective-permute-done((bf16[2048,128]{1,0:T(8,128)(2,1)}, bf16[2048,128]{1,0:T(8,128)(2,1)S(1)}, u32[]{:S(2)}, u32[]{:S(2)}) %collective-permute-start.8) | collective-permute-done | bytes 524320 | tf_op jit(solution)/shard_map/ppermute | solution.py:32
  35.4 1.9 %broadcast_select_fusion = bf16[2048,128]{1,0:T(8,128)(2,1)} fusion(bf16[2048,128]{1,0:T(8,128)(2,1)S(1)} %collective-permute-done.8.refs_3_, pred[]{:T(512)S(6)} %eq.123, bf16[4,4,128,128]{3,2,1,0:T(8,128)(2,1)} %get-tuple-element.17), kind=kLoop, calls=%fused_computation.1 | loop fusion | flops 262144 | bytes 1572865 | tf_op jit(solution)/shard_map/jit(_where)/select_n | solution.py:216
  37.4 5.4 %collective-permute-done.10 = bf16[512,128]{1,0:T(8,128)(2,1)S(1)} collective-permute-done((bf16[512,128]{1,0:T(8,128)(2,1)S(1)}, bf16[512,128]{1,0:T(8,128)(2,1)S(1)}, u32[]{:S(2)}, u32[]{:S(2)}) %collective-permute-start.10) | collective-permute-done | bytes 131104 | tf_op jit(solution)/shard_map/ppermute | solution.py:27
  42.8 2.8 %collective-permute-start.11 = (bf16[1024,128]{1,0:T(8,128)(2,1)S(1)}, bf16[1024,128]{1,0:T(8,128)(2,1)}, u32[]{:S(2)}, u32[]{:S(2)}) collective-permute-start(bf16[1024,128]{1,0:T(8,128)(2,1)S(1)} %pad_maximum_fusion.2.refs_0_), channel_id=1, source_target_pairs={{0,24},{4,28},{8,0},{12,4},{16,8},{20,12},{24,16},{28,20},{1,25},{... | collective-permute-start | bytes 786440 | tf_op jit(solution)/shard_map/ppermute | solution.py:32
  45.6 1.3 %collective-permute-start.12 = (bf16[1024,128]{1,0:T(8,128)(2,1)S(1)}, bf16[1024,128]{1,0:T(8,128)(2,1)}, u32[]{:S(2)}, u32[]{:S(2)}) collective-permute-start(bf16[1024,128]{1,0:T(8,128)(2,1)S(1)} %pad_maximum_fusion.2.refs_0_), channel_id=1, source_target_pairs={{0,16},{4,20},{8,24},{12,28},{16,0},{20,4},{24,8},{28,12},{1,17},{... | collective-permute-start | bytes 786440 | tf_op jit(solution)/shard_map/ppermute | solution.py:32
  46.8 2.8 %collective-permute-start.13 = (bf16[1024,128]{1,0:T(8,128)(2,1)S(1)}, bf16[1024,128]{1,0:T(8,128)(2,1)}, u32[]{:S(2)}, u32[]{:S(2)}) collective-permute-start(bf16[1024,128]{1,0:T(8,128)(2,1)S(1)} %pad_maximum_fusion.2.refs_0_), channel_id=1, source_target_pairs={{0,8},{4,12},{8,16},{12,20},{16,24},{20,28},{24,0},{28,4},{1,9},{5... | collective-permute-start | bytes 786440 | tf_op jit(solution)/shard_map/ppermute | solution.py:32
  49.7 0.1 constant_dynamic-update-slice_fusion
  49.8 1.1 %copy-done.4 = bf16[6272,128]{1,0:T(8,128)(2,1)} copy-done((bf16[6272,128]{1,0:T(8,128)(2,1)}, bf16[6272,128]{1,0:T(8,128)(2,1)S(1)}, u32[]{:S(2)}) %copy-start.4) | copy-done | bytes 1605656
  50.9 0.1 select_reduce_fusion.2
  51.0 0.1 eq.108
  51.1 0.1 select_reduce_fusion.1
  51.3 0.7 slice.40
  52.0 0.1 reshape.205
  52.1 0.2 select_reduce_fusion.3
  52.3 0.1 iota_compare_fusion.1
  52.3 0.1 copy.22
  52.4 0.1 select_n.177
  52.5 0.1 select_reduce_fusion
  52.7 0.1 copy.24
  52.8 0.1 select_n.182
  52.9 0.1 pad_add_fusion.index
  53.0 7.7 %collective-permute-done.9.refs_2_ = bf16[2048,128]{1,0:T(8,128)(2,1)} collective-permute-done((bf16[2048,128]{1,0:T(8,128)(2,1)}, bf16[2048,128]{1,0:T(8,128)(2,1)}, u32[]{:S(2)}, u32[]{:S(2)}) %collective-permute-start.9) | collective-permute-done | bytes 524320 | tf_op jit(solution)/shard_map/ppermute | solution.py:27
  60.7 5.8 %shard_map.55 = (bf16[16,128,512]{2,1,0:T(8,128)(2,1)S(1)}, bf16[16,128,512]{2,1,0:T(8,128)(2,1)}) custom-call(s32[120]{0:T(128)S(1)} %pad_add_fusion.index, bf16[16,4,128,128]{3,2,1,0:T(8,128)(2,1)} %prior.3, bf16[2048,128]{1,0:T(8,128)(2,1)S(1)} %collective-permute-done.7.refs_0_, bf16[2048,128]{1,0:T(8,128)(2,1)S(1)} %collective-permute-done.4.refs_1_, ...), custom_call_target="tpu_custom_call" | custom-call | bytes 8388608 | tf_op jit(solution)/shard_map/pallas_call | solution.py:355
  66.6 0.7 collective-permute-done.13.refs_3_
  67.2 5.5 %shard_map.57 = bf16[16,4,128,128]{3,2,1,0:T(8,128)(2,1)} custom-call(s32[64]{0:T(128)S(1)} %reshape.196.index, bf16[16,4,128,128]{3,2,1,0:T(8,128)(2,1)S(1)} %copy-done, bf16[16,128,512]{2,1,0:T(8,128)(2,1)S(1)} %get-tuple-element.12.first, bf16[16,128,512]{2,1,0:T(8,128)(2,1)} %get-tuple-element.13.second, ...), custom_call_target="tpu_custom_call" | custom-call | flops 1000000000 | bytes 8388608 | tf_op jit(solution)/shard_map/pallas_call | solution.py:380
  (50 shorter events, 0.5 us)
Async XLA Ops:
  0.0 12.6 %copy-start.1 = (bf16[4,2,128,128]{3,2,1,0:T(8,128)(2,1)S(1)}, bf16[4,2,128,128]{3,2,1,0:T(8,128)(2,1)}, u32[]{:S(2)}) copy-start(bf16[4,2,128,128]{3,2,1,0:T(8,128)(2,1)} %param.8) | copy-start | bytes 786436
  0.0 12.6 %copy-start.6 = (s32[4]{0:T(128)S(1)}, s32[4]{0:T(128)}, u32[]{:S(2)}) copy-start(s32[4]{0:T(128)} %param.7) | copy-start | bytes 52
  1.8 12.3 %copy-start.5 = (s32[16,4]{0,1:T(4,128)S(1)}, s32[16,4]{0,1:T(4,128)}, u32[]{:S(2)}) copy-start(s32[16,4]{0,1:T(4,128)} %param.6) | copy-start | bytes 772
  1.8 14.3 %collective-permute-start = (bf16[528,128]{1,0:T(8,128)(2,1)S(1)}, bf16[528,128]{1,0:T(8,128)(2,1)S(1)}, u32[]{:S(2)}, u32[]{:S(2)}) collective-permute-start(bf16[528,128]{1,0:T(8,128)(2,1)S(1)} %fusion.2), channel_id=1, source_target_pairs={{6,2},{7,3},{10,6},{11,7},{14,10},{15,11},{18,14},{19,15},{22,18},... | collective-permute-start | bytes 405512 | tf_op jit(solution)/shard_map/ppermute | solution.py:238
  5.2 11.0 %collective-permute-start.1 = (bf16[528,128]{1,0:T(8,128)(2,1)S(1)}, bf16[528,128]{1,0:T(8,128)(2,1)S(1)}, u32[]{:S(2)}, u32[]{:S(2)}) collective-permute-start(bf16[528,128]{1,0:T(8,128)(2,1)S(1)} %fusion.3), channel_id=1, source_target_pairs={{6,0},{7,1},{10,4},{11,5},{14,8},{15,9},{18,12},{19,13},{22,16},{2... | collective-permute-start | bytes 405512 | tf_op jit(solution)/shard_map/ppermute | solution.py:239
  8.5 16.7 %collective-permute-start.4 = (bf16[2048,128]{1,0:T(8,128)(2,1)S(1)}, bf16[2048,128]{1,0:T(8,128)(2,1)S(1)}, u32[]{:S(2)}, u32[]{:S(2)}) collective-permute-start(bf16[2048,128]{1,0:T(8,128)(2,1)S(1)} %bitcast.25), channel_id=1, source_target_pairs={{0,24},{4,28},{8,0},{12,4},{16,8},{20,12},{24,16},{28,20},{1,25},{... | collective-permute-start | bytes 1572872 | tf_op jit(solution)/shard_map/ppermute | solution.py:32
  12.2 23.2 %collective-permute-start.8 = (bf16[2048,128]{1,0:T(8,128)(2,1)}, bf16[2048,128]{1,0:T(8,128)(2,1)S(1)}, u32[]{:S(2)}, u32[]{:S(2)}) collective-permute-start(bf16[2048,128]{1,0:T(8,128)(2,1)} %bitcast.9), channel_id=1, source_target_pairs={{0,24},{4,28},{8,0},{12,4},{16,8},{20,12},{24,16},{28,20},{1,25},{... | collective-permute-start | bytes 1572872 | tf_op jit(solution)/shard_map/ppermute | solution.py:32
  16.9 12.6 %collective-permute-start.2 = (bf16[1568,128]{1,0:T(8,128)(2,1)S(1)}, bf16[1568,128]{1,0:T(8,128)(2,1)S(1)}, u32[]{:S(2)}, u32[]{:S(2)}) collective-permute-start(bf16[1568,128]{1,0:T(8,128)(2,1)S(1)} %pad_maximum_fusion.1.refs_4_), channel_id=1, source_target_pairs={{0,2},{1,3},{2,0},{3,1},{4,6},{5,7},{6,4},{7,5},{8,10},{9,11},{10,... | collective-permute-start | bytes 1204232 | tf_op jit(solution)/shard_map/ppermute | solution.py:27
  25.3 12.0 %collective-permute-start.5 = (s32[8,4]{0,1:T(4,128)S(1)}, s32[8,4]{0,1:T(4,128)S(1)}, u32[]{:S(2)}, u32[]{:S(2)}) collective-permute-start(s32[8,4]{0,1:T(4,128)S(1)} %slice.35), channel_id=1, source_target_pairs={{0,28},{4,0},{8,4},{12,8},{16,12},{20,16},{24,20},{28,24},{1,29},{... | collective-permute-start | bytes 392 | tf_op jit(solution)/shard_map/ppermute | solution.py:32
  25.3 27.3 %collective-permute-start.6 = (s32[8,4]{0,1:T(4,128)S(1)}, s32[8,4]{0,1:T(4,128)S(1)}, u32[]{:S(2)}, u32[]{:S(2)}) collective-permute-start(s32[8,4]{0,1:T(4,128)S(1)} %slice.35), channel_id=1, source_target_pairs={{0,24},{4,28},{8,0},{12,4},{16,8},{20,12},{24,16},{28,20},{1,25},{... | collective-permute-start | bytes 392 | tf_op jit(solution)/shard_map/ppermute | solution.py:32
  29.4 7.9 %copy-start.2 = (bf16[4,128,128]{2,1,0:T(8,128)(2,1)S(1)}, bf16[4,128,128]{2,1,0:T(8,128)(2,1)}, u32[]{:S(2)}) copy-start(bf16[4,128,128]{2,1,0:T(8,128)(2,1)} %shard_map.56) | copy-start | bytes 393220
  29.4 7.9 %copy-start.3 = (bf16[6272,128]{1,0:T(8,128)(2,1)S(1)}, bf16[6272,128]{1,0:T(8,128)(2,1)}, u32[]{:S(2)}) copy-start(bf16[6272,128]{1,0:T(8,128)(2,1)} %get-tuple-element.15) | copy-start | bytes 4816900
  29.4 17.4 %collective-permute-start.7 = (bf16[2048,128]{1,0:T(8,128)(2,1)S(1)}, bf16[2048,128]{1,0:T(8,128)(2,1)S(1)}, u32[]{:S(2)}, u32[]{:S(2)}) collective-permute-start(bf16[2048,128]{1,0:T(8,128)(2,1)S(1)} %broadcast_select_fusion.1), channel_id=1, source_target_pairs={{0,4},{4,0},{8,12},{12,8},{16,20},{20,16},{24,28},{28,24},{1,5},{5... | collective-permute-start | bytes 1572872 | tf_op jit(solution)/shard_map/ppermute | solution.py:27
  29.6 20.1 %collective-permute-start.3 = (bf16[3136,128]{1,0:T(8,128)(2,1)S(1)}, bf16[3136,128]{1,0:T(8,128)(2,1)S(1)}, u32[]{:S(2)}, u32[]{:S(2)}) collective-permute-start(bf16[3136,128]{1,0:T(8,128)(2,1)S(1)} %pad_maximum_fusion), channel_id=1, source_target_pairs={{0,1},{1,0},{2,3},{3,2},{4,5},{5,4},{6,7},{7,6},{8,9},{9,8},{10,11... | collective-permute-start | bytes 2408456 | tf_op jit(solution)/shard_map/ppermute | solution.py:27
  37.3 5.5 %collective-permute-start.10 = (bf16[512,128]{1,0:T(8,128)(2,1)S(1)}, bf16[512,128]{1,0:T(8,128)(2,1)S(1)}, u32[]{:S(2)}, u32[]{:S(2)}) collective-permute-start(bf16[512,128]{1,0:T(8,128)(2,1)S(1)} %bitcast.26), channel_id=1, source_target_pairs={{0,4},{4,0},{8,12},{12,8},{16,20},{20,16},{24,28},{28,24},{1,5},{5... | collective-permute-start | bytes 393224 | tf_op jit(solution)/shard_map/ppermute | solution.py:27
  42.8 23.7 %collective-permute-start.11 = (bf16[1024,128]{1,0:T(8,128)(2,1)S(1)}, bf16[1024,128]{1,0:T(8,128)(2,1)}, u32[]{:S(2)}, u32[]{:S(2)}) collective-permute-start(bf16[1024,128]{1,0:T(8,128)(2,1)S(1)} %pad_maximum_fusion.2.refs_0_), channel_id=1, source_target_pairs={{0,24},{4,28},{8,0},{12,4},{16,8},{20,12},{24,16},{28,20},{1,25},{... | collective-permute-start | bytes 786440 | tf_op jit(solution)/shard_map/ppermute | solution.py:32
  45.6 21.0 %collective-permute-start.12 = (bf16[1024,128]{1,0:T(8,128)(2,1)S(1)}, bf16[1024,128]{1,0:T(8,128)(2,1)}, u32[]{:S(2)}, u32[]{:S(2)}) collective-permute-start(bf16[1024,128]{1,0:T(8,128)(2,1)S(1)} %pad_maximum_fusion.2.refs_0_), channel_id=1, source_target_pairs={{0,16},{4,20},{8,24},{12,28},{16,0},{20,4},{24,8},{28,12},{1,17},{... | collective-permute-start | bytes 786440 | tf_op jit(solution)/shard_map/ppermute | solution.py:32
  46.8 20.4 %collective-permute-start.13 = (bf16[1024,128]{1,0:T(8,128)(2,1)S(1)}, bf16[1024,128]{1,0:T(8,128)(2,1)}, u32[]{:S(2)}, u32[]{:S(2)}) collective-permute-start(bf16[1024,128]{1,0:T(8,128)(2,1)S(1)} %pad_maximum_fusion.2.refs_0_), channel_id=1, source_target_pairs={{0,8},{4,12},{8,16},{12,20},{16,24},{20,28},{24,0},{28,4},{1,9},{5... | collective-permute-start | bytes 786440 | tf_op jit(solution)/shard_map/ppermute | solution.py:32
  49.7 11.1 %collective-permute-start.9 = (bf16[2048,128]{1,0:T(8,128)(2,1)}, bf16[2048,128]{1,0:T(8,128)(2,1)}, u32[]{:S(2)}, u32[]{:S(2)}) collective-permute-start(bf16[2048,128]{1,0:T(8,128)(2,1)} %broadcast_select_fusion), channel_id=1, source_target_pairs={{0,4},{4,0},{8,12},{12,8},{16,20},{20,16},{24,28},{28,24},{1,5},{5... | collective-permute-start | bytes 1572872 | tf_op jit(solution)/shard_map/ppermute | solution.py:27
  49.8 1.2 %copy-start.4 = (bf16[6272,128]{1,0:T(8,128)(2,1)}, bf16[6272,128]{1,0:T(8,128)(2,1)S(1)}, u32[]{:S(2)}) copy-start(bf16[6272,128]{1,0:T(8,128)(2,1)S(1)} %constant_dynamic-update-slice_fusion) | copy-start | bytes 4816900
  53.0 14.2 %copy-start = (bf16[16,4,128,128]{3,2,1,0:T(8,128)(2,1)S(1)}, bf16[16,4,128,128]{3,2,1,0:T(8,128)(2,1)}, u32[]{:S(2)}) copy-start(bf16[16,4,128,128]{3,2,1,0:T(8,128)(2,1)} %prior.3) | copy-start | bytes 6291460

commit v3 on v2

--- a/solution.py
+++ b/solution.py
@@ -10,12 +10,13 @@
 mixing = 0.75
 pad = 16
 plan = {'sizes': (4, 4),
- 'gates': {'Y1': ['Y0'], 'T': ['I1'], 'I1': ['Z0'], 'I2': ['Z0']},
- 'order': ['Z0', 'I', 'Z1', 'T', 'KM', 'Y0', 'X', 'Y1', 'E1', 'E2', 'E3'],
+ 'gates': {'Y1': ['Y0'], 'T': ['Z0'], 'I1': ['T'], 'I2': ['T'], 'E1': ['Y0'], 'E3': ['Y0']},
+ 'order': ['Z0', 'Z1', 'KM', 'T', 'I', 'X', 'Y0', 'Y1', 'E1', 'E2', 'E3'],
  'cost': 0,
  'groups': 4,
  'vmem': 48,
- 'any': True}
+ 'any': True,
+ 'parts_later': False}
 
 
 def bits_of(count):
@@ -92,8 +93,20 @@
     zero = jnp.zeros((block, block), jnp.bfloat16)
     for ref in (p1, p2, first_next):
         ref[pl.ds(count * block, block), :] = zero
-    for copy in copies:
-        copy.wait()
+    for copy, (_, _, _, which, _) in zip(copies, layout):
+        if which != 1:
+            copy.wait()
+    for i in range(rows):
+        own = side([prior[i, k] for k in range(per_quarter)])
+        cross = side([blk(p1, index[at_pick + i * per_quarter + k]) for k in range(per_quarter)])
+        first[i] = jnp.dot(
+            row_weights(index[i]),
+            jnp.concatenate([own, cross], axis=0),
+            preferred_element_type=jnp.float32,
+        ).astype(jnp.bfloat16)
+    for copy, (_, _, _, which, _) in zip(copies, layout):
+        if which == 1:
+            copy.wait()
     for j in range(half):
         top = side([blk(p1, j * per_quarter + k) for k in range(per_quarter)])
         low = side([blk(p2, index[at_pick_next + j * per_quarter + k]) for k in range(per_quarter)])
@@ -104,14 +117,6 @@
         ).astype(jnp.bfloat16)
         for k in range(per_quarter):
             first_next[pl.ds((j * per_quarter + k) * block, block), :] = got[:, k * block : (k + 1) * block]
-    for i in range(rows):
-        own = side([prior[i, k] for k in range(per_quarter)])
-        cross = side([blk(p1, index[at_pick + i * per_quarter + k]) for k in range(per_quarter)])
-        first[i] = jnp.dot(
-            row_weights(index[i]),
-            jnp.concatenate([own, cross], axis=0),
-            preferred_element_type=jnp.float32,
-        ).astype(jnp.bfloat16)
     for i in range(rows):
         cross = side([blk(first_next, index[at_pick + i * per_quarter + k]) for k in range(per_quarter)])
         second[i] = jnp.dot(
@@ -175,7 +180,7 @@
     there = {}
 
     def gated(array, name):
-        return after(array, *[there[n] for n in plan["gates"].get(name, ())])
+        return after(array, *[there[n] for n in plan["gates"].get(name, ()) if n in there])
 
     def record(name, array):
         there[name] = array
@@ -200,6 +205,8 @@
         )
         for c in range(2)
     ]
+    if plan["parts_later"]:
+        parts = [after(array, *mine) for array in parts]
     turned = pl.pallas_call(
         transpose_kernel, out_shape=jax.ShapeDtypeStruct(a2_blocks.shape, a2_blocks.dtype)
     )(a2_blocks).reshape(-1, block)
@@ -345,11 +352,13 @@
     for c in range(chunks):
         size = sizes[c] * per_quarter * block
         piece(near[c], 0, size, 0, starts[c] * per_quarter * block)
-        piece(far[c], 0, size, 1, starts[c] * per_quarter * block)
     to = 0
     for array in w["pieces"]:
         piece(array, 0, array.shape[0], 2, to)
         to += array.shape[0]
+    for c in range(chunks):
+        size = sizes[c] * per_quarter * block
+        piece(far[c], 0, size, 1, starts[c] * per_quarter * block)
     wide = jax.ShapeDtypeStruct((rows, block, per_quarter * block), jnp.bfloat16)
     stack = pltpu.VMEM(((count + 1) * block, block), jnp.bfloat16)
     first, second = pl.pallas_call(

time: 74.2 us -> 71.4 us (0.962); the launches traced: 72.7 us -> 70.9 us
  waiting for transfers between devices: 27.8 us -> 25.1 us
    ppermute x5, waiting for transfers between devices: 13.1 us -> 8.46 us  [exchange(): return lax.ppermute(array, axis, [(i, i ^ mask) for i in range(count)])]
    ppermute x5, starting transfers between devices: 0.22 us -> 4.25 us  [exchange(): return lax.ppermute(array, axis, [(i, i ^ mask) for i in range(count)])]
    ppermute x7, starting transfers between devices: 15 us -> 11.6 us  [taken_from(): lax.ppermute(array, axis, [(i, (i - ahead) % count) for i in range(count)])]
    ppermute x7, waiting for transfers between devices: 14.7 us -> 16.7 us  [taken_from(): lax.ppermute(array, axis, [(i, (i - ahead) % count) for i in range(count)])]
  transfers between devices with their start and end apart: 14 -> 14, of which waited for: 5 -> 4; matrix products, arithmetic and copies ran while one was open for 12% -> 13% of each run, Pallas kernels for 10% -> 11%
where the time goes in v3:
time: 71.4 us; the launch traced here: 70.9 us
  waiting for transfers between devices  25.1 us (35%)
  starting transfers between devices  20.5 us (29%)
  Pallas kernels  13.2 us (18%)
  local copies, waits for them, and re-layouts  7.4 us (10%)
  other arithmetic  4.49 us (6%)
    ppermute x7, waiting for transfers between devices, taken_from(): lax.ppermute(array, axis, [(i, (i - ahead) % count) for i in range(count)])  16.7 us
    ppermute x7, starting transfers between devices, taken_from(): lax.ppermute(array, axis, [(i, (i - ahead) % count) for i in range(count)])  11.6 us
    ppermute x5, waiting for transfers between devices, exchange(): return lax.ppermute(array, axis, [(i, i ^ mask) for i in range(count)])  8.46 us
    pallas_call x1, Pallas kernels, local(): pl.pallas_call(functools.partial(left_kernel, tuple(layout), rows, per_qu...  6.07 us
    pallas_call x1, Pallas kernels, local(): pl.pallas_call(functools.partial(right_kernel, tuple(layout), rows, per_q...  5.49 us
    ppermute x5, starting transfers between devices, exchange(): return lax.ppermute(array, axis, [(i, i ^ mask) for i in range(count)])  4.25 us
    ppermute x1, starting transfers between devices, do_next(): w['kept'] = record('K', lax.ppermute(gated(parts[0], 'K'), both, kept))  3.31 us
    slice x1, local copies, waits for them, and re-layouts, local(): prior[half + starts[c]:half + starts[c] + sizes[c]].reshape(-1, block)  2.09 us
  transfers between devices with their start and end apart: 14, of which 4 were waited for; matrix products, arithmetic and copies ran while one was open for 13% of the time, Pallas kernels for 11%

profile of v3, /device:TPU:10, one launch (start us, length us, event | category | flops | bytes accessed | tf_op | source)
XLA Modules:
  0.0 70.9 jit_solution(13498540389756289136)
XLA Ops:
  0.0 1.0 %fusion.21 = (bf16[2,2,128,128]{3,2,1,0:T(8,128)(2,1)S(1)}, bf16[2,2,128,128]{3,2,1,0:T(8,128)(2,1)S(1)}) fusion(bf16[4,2,128,128]{3,2,1,0:T(8,128)(2,1)} %param.8), kind=kLoop, calls=%fused_computation.84 | loop fusion | bytes 524288 | tf_op jit(solution)/shard_map/slice | solution.py:203
  1.1 0.7 fusion.17
  1.7 0.1 slice_bitcast_fusion
  1.8 3.3 %collective-permute-start = (bf16[528,128]{1,0:T(8,128)(2,1)S(1)}, bf16[528,128]{1,0:T(8,128)(2,1)S(1)}, u32[]{:S(2)}, u32[]{:S(2)}) collective-permute-start(bf16[528,128]{1,0:T(8,128)(2,1)S(1)} %fusion.2), channel_id=1, source_target_pairs={{6,2},{7,3},{10,6},{11,7},{14,10},{15,11},{18,14},{19,15},{22,18},... | collective-permute-start | bytes 405512 | tf_op jit(solution)/shard_map/ppermute | solution.py:245
  5.2 1.3 %collective-permute-start.1 = (bf16[528,128]{1,0:T(8,128)(2,1)S(1)}, bf16[528,128]{1,0:T(8,128)(2,1)S(1)}, u32[]{:S(2)}, u32[]{:S(2)}) collective-permute-start(bf16[528,128]{1,0:T(8,128)(2,1)S(1)} %fusion.3), channel_id=1, source_target_pairs={{6,0},{7,1},{10,4},{11,5},{14,8},{15,9},{18,12},{19,13},{22,16},{2... | collective-permute-start | bytes 405512 | tf_op jit(solution)/shard_map/ppermute | solution.py:246
  6.5 2.1 %fusion.20 = (bf16[4,4,128,128]{3,2,1,0:T(8,128)(2,1)}, bf16[4,4,128,128]{3,2,1,0:T(8,128)(2,1)S(1)}) fusion(bf16[16,4,128,128]{3,2,1,0:T(8,128)(2,1)} %prior.3), kind=kLoop, calls=%fused_computation.83 | loop fusion | bytes 2097152 | tf_op jit(solution)/shard_map/slice | solution.py:197
  8.5 3.6 %collective-permute-start.4 = (bf16[2048,128]{1,0:T(8,128)(2,1)S(1)}, bf16[2048,128]{1,0:T(8,128)(2,1)S(1)}, u32[]{:S(2)}, u32[]{:S(2)}) collective-permute-start(bf16[2048,128]{1,0:T(8,128)(2,1)S(1)} %bitcast.25), channel_id=1, source_target_pairs={{0,24},{4,28},{8,0},{12,4},{16,8},{20,12},{24,16},{28,20},{1,25},{... | collective-permute-start | bytes 1572872 | tf_op jit(solution)/shard_map/ppermute | solution.py:33
  12.2 0.4 collective-permute-start.9
  12.6 0.7 %constant_dynamic-update-slice_fusion.4 = bf16[6272,128]{1,0:T(8,128)(2,1)} fusion(bf16[1024,128]{1,0:T(8,128)(2,1)S(1)} %bitcast.22), kind=kLoop, calls=%fused_computation.17 | loop fusion | bytes 524288
  13.4 0.1 iota_compare_fusion.4
  13.4 0.6 fusion.22
  14.2 0.1 slice.35
  14.2 1.6 %shard_map.55 = bf16[4,128,128]{2,1,0:T(8,128)(2,1)} custom-call(bf16[4,128,128]{2,1,0:T(8,128)(2,1)} %src.1), custom_call_target="tpu_custom_call" | custom-call | tf_op jit(solution)/shard_map/pallas_call | solution.py:210
  15.9 0.1 add.149
  16.0 0.1 copy.20
  16.0 0.1 reshape.196.index
  16.2 0.7 constant_dynamic-update-slice_fusion.2
  16.9 0.1 collective-permute-start.2
  17.0 8.3 %collective-permute-done.4.refs_5_ = bf16[2048,128]{1,0:T(8,128)(2,1)S(1)} collective-permute-done((bf16[2048,128]{1,0:T(8,128)(2,1)S(1)}, bf16[2048,128]{1,0:T(8,128)(2,1)S(1)}, u32[]{:S(2)}, u32[]{:S(2)}) %collective-permute-start.4) | collective-permute-done | bytes 524320 | tf_op jit(solution)/shard_map/ppermute | solution.py:33
  25.3 0.1 broadcast_select_fusion.1
  25.4 2.1 %collective-permute-start.8 = (bf16[2048,128]{1,0:T(8,128)(2,1)S(1)}, bf16[2048,128]{1,0:T(8,128)(2,1)S(1)}, u32[]{:S(2)}, u32[]{:S(2)}) collective-permute-start(bf16[2048,128]{1,0:T(8,128)(2,1)S(1)} %broadcast_select_fusion.1), channel_id=1, source_target_pairs={{0,4},{4,0},{8,12},{12,8},{16,20},{20,16},{24,28},{28,24},{1,5},{5... | collective-permute-start | bytes 1572872 | tf_op jit(solution)/shard_map/ppermute | solution.py:28
  27.5 0.1 collective-permute-start.3
  27.6 7.7 %collective-permute-done.9.refs_6_ = bf16[2048,128]{1,0:T(8,128)(2,1)S(1)} collective-permute-done((bf16[2048,128]{1,0:T(8,128)(2,1)}, bf16[2048,128]{1,0:T(8,128)(2,1)S(1)}, u32[]{:S(2)}, u32[]{:S(2)}) %collective-permute-start.9) | collective-permute-done | bytes 524320 | tf_op jit(solution)/shard_map/ppermute | solution.py:33
  35.4 1.9 %broadcast_select_fusion = bf16[2048,128]{1,0:T(8,128)(2,1)} fusion(bf16[2048,128]{1,0:T(8,128)(2,1)S(1)} %collective-permute-done.9.refs_6_, pred[]{:T(512)S(6)} %eq.123, bf16[4,4,128,128]{3,2,1,0:T(8,128)(2,1)} %get-tuple-element.19), kind=kLoop, calls=%fused_computation.1 | loop fusion | flops 262144 | bytes 1572865 | tf_op jit(solution)/shard_map/jit(_where)/select_n | solution.py:223
  37.4 3.7 %collective-permute-start.7 = (s32[8,4]{0,1:T(4,128)S(1)}, s32[8,4]{0,1:T(4,128)S(1)}, u32[]{:S(2)}, u32[]{:S(2)}) collective-permute-start(s32[8,4]{0,1:T(4,128)S(1)} %slice.35), channel_id=1, source_target_pairs={{0,24},{4,28},{8,0},{12,4},{16,8},{20,12},{24,16},{28,20},{1,25},{... | collective-permute-start | bytes 392 | tf_op jit(solution)/shard_map/ppermute | solution.py:33
  41.1 0.8 %collective-permute-start.12 = (bf16[1024,128]{1,0:T(8,128)(2,1)S(1)}, bf16[1024,128]{1,0:T(8,128)(2,1)}, u32[]{:S(2)}, u32[]{:S(2)}) collective-permute-start(bf16[1024,128]{1,0:T(8,128)(2,1)S(1)} %pad_maximum_fusion.2.refs_0_), channel_id=1, source_target_pairs={{0,16},{4,20},{8,24},{12,28},{16,0},{20,4},{24,8},{28,12},{1,17},{... | collective-permute-start | bytes 786440 | tf_op jit(solution)/shard_map/ppermute | solution.py:33
  41.9 1.5 %collective-permute-start.11 = (bf16[1024,128]{1,0:T(8,128)(2,1)S(1)}, bf16[1024,128]{1,0:T(8,128)(2,1)}, u32[]{:S(2)}, u32[]{:S(2)}) collective-permute-start(bf16[1024,128]{1,0:T(8,128)(2,1)S(1)} %pad_maximum_fusion.2.refs_0_), channel_id=1, source_target_pairs={{0,24},{4,28},{8,0},{12,4},{16,8},{20,12},{24,16},{28,20},{1,25},{... | collective-permute-start | bytes 786440 | tf_op jit(solution)/shard_map/ppermute | solution.py:33
  43.5 1.4 %collective-permute-start.13 = (bf16[1024,128]{1,0:T(8,128)(2,1)S(1)}, bf16[1024,128]{1,0:T(8,128)(2,1)}, u32[]{:S(2)}, u32[]{:S(2)}) collective-permute-start(bf16[1024,128]{1,0:T(8,128)(2,1)S(1)} %pad_maximum_fusion.2.refs_0_), channel_id=1, source_target_pairs={{0,8},{4,12},{8,16},{12,20},{16,24},{20,28},{24,0},{28,4},{1,9},{5... | collective-permute-start | bytes 786440 | tf_op jit(solution)/shard_map/ppermute | solution.py:33
  44.9 0.1 constant_dynamic-update-slice_fusion
  45.0 1.1 %copy-done.4 = bf16[6272,128]{1,0:T(8,128)(2,1)} copy-done((bf16[6272,128]{1,0:T(8,128)(2,1)}, bf16[6272,128]{1,0:T(8,128)(2,1)S(1)}, u32[]{:S(2)}) %copy-start.4) | copy-done | bytes 1605656
  46.2 0.1 select_reduce_fusion.2
  46.3 0.1 eq.108
  46.4 2.0 %collective-permute-start.10 = (bf16[2048,128]{1,0:T(8,128)(2,1)}, bf16[2048,128]{1,0:T(8,128)(2,1)}, u32[]{:S(2)}, u32[]{:S(2)}) collective-permute-start(bf16[2048,128]{1,0:T(8,128)(2,1)} %broadcast_select_fusion), channel_id=1, source_target_pairs={{0,4},{4,0},{8,12},{12,8},{16,20},{20,16},{24,28},{28,24},{1,5},{5... | collective-permute-start | bytes 1572872 | tf_op jit(solution)/shard_map/ppermute | solution.py:28
  48.4 0.1 select_reduce_fusion.1
  48.5 0.7 slice.40
  49.2 0.1 reshape.205
  49.3 0.2 select_reduce_fusion.3
  49.5 0.1 iota_compare_fusion.1
  49.6 0.1 copy.22
  49.7 0.1 select_n.177
  49.8 0.1 select_reduce_fusion
  50.0 0.1 copy.24
  50.1 0.1 select_n.182
  50.2 0.1 pad_add_fusion.index
  50.3 8.5 %collective-permute-done.10.refs_1_ = bf16[2048,128]{1,0:T(8,128)(2,1)} collective-permute-done((bf16[2048,128]{1,0:T(8,128)(2,1)}, bf16[2048,128]{1,0:T(8,128)(2,1)}, u32[]{:S(2)}, u32[]{:S(2)}) %collective-permute-start.10) | collective-permute-done | bytes 524320 | tf_op jit(solution)/shard_map/ppermute | solution.py:28
  58.7 6.1 %shard_map.56 = (bf16[16,128,512]{2,1,0:T(8,128)(2,1)S(1)}, bf16[16,128,512]{2,1,0:T(8,128)(2,1)}) custom-call(s32[120]{0:T(128)S(1)} %pad_add_fusion.index, bf16[16,4,128,128]{3,2,1,0:T(8,128)(2,1)} %prior.3, bf16[2048,128]{1,0:T(8,128)(2,1)S(1)} %collective-permute-done.8.refs_0_, bf16[2048,128]{1,0:T(8,128)(2,1)} %collective-permute-done.10.refs_1_, ...), custom_call_target="tpu_custom_call" | custom-call | bytes 8388608 | tf_op jit(solution)/shard_map/pallas_call | solution.py:364
  64.8 0.6 collective-permute-done.11.refs_1_
  65.4 5.5 %shard_map.57 = bf16[16,4,128,128]{3,2,1,0:T(8,128)(2,1)} custom-call(s32[64]{0:T(128)S(1)} %reshape.196.index, bf16[16,4,128,128]{3,2,1,0:T(8,128)(2,1)S(1)} %copy-done, bf16[16,128,512]{2,1,0:T(8,128)(2,1)S(1)} %get-tuple-element.14.first, bf16[16,128,512]{2,1,0:T(8,128)(2,1)} %get-tuple-element.15.second, ...), custom_call_target="tpu_custom_call" | custom-call | flops 1000000000 | bytes 8388608 | tf_op jit(solution)/shard_map/pallas_call | solution.py:389
  (50 shorter events, 0.6 us)
Async XLA Ops:
  0.0 12.6 %copy-start.1 = (bf16[4,2,128,128]{3,2,1,0:T(8,128)(2,1)S(1)}, bf16[4,2,128,128]{3,2,1,0:T(8,128)(2,1)}, u32[]{:S(2)}) copy-start(bf16[4,2,128,128]{3,2,1,0:T(8,128)(2,1)} %param.8) | copy-start | bytes 786436
  0.0 12.6 %copy-start.6 = (s32[4]{0:T(128)S(1)}, s32[4]{0:T(128)}, u32[]{:S(2)}) copy-start(s32[4]{0:T(128)} %param.7) | copy-start | bytes 52
  1.8 12.3 %copy-start.5 = (s32[16,4]{0,1:T(4,128)S(1)}, s32[16,4]{0,1:T(4,128)}, u32[]{:S(2)}) copy-start(s32[16,4]{0,1:T(4,128)} %param.6) | copy-start | bytes 772
  1.8 14.3 %collective-permute-start = (bf16[528,128]{1,0:T(8,128)(2,1)S(1)}, bf16[528,128]{1,0:T(8,128)(2,1)S(1)}, u32[]{:S(2)}, u32[]{:S(2)}) collective-permute-start(bf16[528,128]{1,0:T(8,128)(2,1)S(1)} %fusion.2), channel_id=1, source_target_pairs={{6,2},{7,3},{10,6},{11,7},{14,10},{15,11},{18,14},{19,15},{22,18},... | collective-permute-start | bytes 405512 | tf_op jit(solution)/shard_map/ppermute | solution.py:245
  5.2 11.0 %collective-permute-start.1 = (bf16[528,128]{1,0:T(8,128)(2,1)S(1)}, bf16[528,128]{1,0:T(8,128)(2,1)S(1)}, u32[]{:S(2)}, u32[]{:S(2)}) collective-permute-start(bf16[528,128]{1,0:T(8,128)(2,1)S(1)} %fusion.3), channel_id=1, source_target_pairs={{6,0},{7,1},{10,4},{11,5},{14,8},{15,9},{18,12},{19,13},{22,16},{2... | collective-permute-start | bytes 405512 | tf_op jit(solution)/shard_map/ppermute | solution.py:246
  8.5 16.7 %collective-permute-start.4 = (bf16[2048,128]{1,0:T(8,128)(2,1)S(1)}, bf16[2048,128]{1,0:T(8,128)(2,1)S(1)}, u32[]{:S(2)}, u32[]{:S(2)}) collective-permute-start(bf16[2048,128]{1,0:T(8,128)(2,1)S(1)} %bitcast.25), channel_id=1, source_target_pairs={{0,24},{4,28},{8,0},{12,4},{16,8},{20,12},{24,16},{28,20},{1,25},{... | collective-permute-start | bytes 1572872 | tf_op jit(solution)/shard_map/ppermute | solution.py:33
  12.2 23.2 %collective-permute-start.9 = (bf16[2048,128]{1,0:T(8,128)(2,1)}, bf16[2048,128]{1,0:T(8,128)(2,1)S(1)}, u32[]{:S(2)}, u32[]{:S(2)}) collective-permute-start(bf16[2048,128]{1,0:T(8,128)(2,1)} %bitcast.10), channel_id=1, source_target_pairs={{0,24},{4,28},{8,0},{12,4},{16,8},{20,12},{24,16},{28,20},{1,25},{... | collective-permute-start | bytes 1572872 | tf_op jit(solution)/shard_map/ppermute | solution.py:33
  16.9 10.6 %collective-permute-start.2 = (bf16[1568,128]{1,0:T(8,128)(2,1)S(1)}, bf16[1568,128]{1,0:T(8,128)(2,1)S(1)}, u32[]{:S(2)}, u32[]{:S(2)}) collective-permute-start(bf16[1568,128]{1,0:T(8,128)(2,1)S(1)} %pad_maximum_fusion.1.refs_2_), channel_id=1, source_target_pairs={{0,2},{1,3},{2,0},{3,1},{4,6},{5,7},{6,4},{7,5},{8,10},{9,11},{10,... | collective-permute-start | bytes 1204232 | tf_op jit(solution)/shard_map/ppermute | solution.py:28
  25.3 12.0 %collective-permute-start.5 = (bf16[512,128]{1,0:T(8,128)(2,1)}, bf16[512,128]{1,0:T(8,128)(2,1)S(1)}, u32[]{:S(2)}, u32[]{:S(2)}) collective-permute-start(bf16[512,128]{1,0:T(8,128)(2,1)} %bitcast.26), channel_id=1, source_target_pairs={{0,4},{4,0},{8,12},{12,8},{16,20},{20,16},{24,28},{28,24},{1,5},{5... | collective-permute-start | bytes 393224 | tf_op jit(solution)/shard_map/ppermute | solution.py:28
  25.4 11.9 %copy-start.3 = (bf16[6272,128]{1,0:T(8,128)(2,1)S(1)}, bf16[6272,128]{1,0:T(8,128)(2,1)}, u32[]{:S(2)}) copy-start(bf16[6272,128]{1,0:T(8,128)(2,1)} %get-tuple-element.17) | copy-start | bytes 4816900
  25.4 15.7 %copy-start.2 = (bf16[4,128,128]{2,1,0:T(8,128)(2,1)S(1)}, bf16[4,128,128]{2,1,0:T(8,128)(2,1)}, u32[]{:S(2)}) copy-start(bf16[4,128,128]{2,1,0:T(8,128)(2,1)} %shard_map.55) | copy-start | bytes 393220
  25.4 16.6 %collective-permute-start.8 = (bf16[2048,128]{1,0:T(8,128)(2,1)S(1)}, bf16[2048,128]{1,0:T(8,128)(2,1)S(1)}, u32[]{:S(2)}, u32[]{:S(2)}) collective-permute-start(bf16[2048,128]{1,0:T(8,128)(2,1)S(1)} %broadcast_select_fusion.1), channel_id=1, source_target_pairs={{0,4},{4,0},{8,12},{12,8},{16,20},{20,16},{24,28},{28,24},{1,5},{5... | collective-permute-start | bytes 1572872 | tf_op jit(solution)/shard_map/ppermute | solution.py:28
  27.5 15.9 %collective-permute-start.3 = (bf16[3136,128]{1,0:T(8,128)(2,1)S(1)}, bf16[3136,128]{1,0:T(8,128)(2,1)S(1)}, u32[]{:S(2)}, u32[]{:S(2)}) collective-permute-start(bf16[3136,128]{1,0:T(8,128)(2,1)S(1)} %pad_maximum_fusion), channel_id=1, source_target_pairs={{0,1},{1,0},{2,3},{3,2},{4,5},{5,4},{6,7},{7,6},{8,9},{9,8},{10,11... | collective-permute-start | bytes 2408456 | tf_op jit(solution)/shard_map/ppermute | solution.py:28
  37.3 9.1 %collective-permute-start.6 = (s32[8,4]{0,1:T(4,128)S(1)}, s32[8,4]{0,1:T(4,128)S(1)}, u32[]{:S(2)}, u32[]{:S(2)}) collective-permute-start(s32[8,4]{0,1:T(4,128)S(1)} %slice.35), channel_id=1, source_target_pairs={{0,28},{4,0},{8,4},{12,8},{16,12},{20,16},{24,20},{28,24},{1,29},{... | collective-permute-start | bytes 392 | tf_op jit(solution)/shard_map/ppermute | solution.py:33
  37.4 12.4 %collective-permute-start.7 = (s32[8,4]{0,1:T(4,128)S(1)}, s32[8,4]{0,1:T(4,128)S(1)}, u32[]{:S(2)}, u32[]{:S(2)}) collective-permute-start(s32[8,4]{0,1:T(4,128)S(1)} %slice.35), channel_id=1, source_target_pairs={{0,24},{4,28},{8,0},{12,4},{16,8},{20,12},{24,16},{28,20},{1,25},{... | collective-permute-start | bytes 392 | tf_op jit(solution)/shard_map/ppermute | solution.py:33
  41.1 23.7 %collective-permute-start.12 = (bf16[1024,128]{1,0:T(8,128)(2,1)S(1)}, bf16[1024,128]{1,0:T(8,128)(2,1)}, u32[]{:S(2)}, u32[]{:S(2)}) collective-permute-start(bf16[1024,128]{1,0:T(8,128)(2,1)S(1)} %pad_maximum_fusion.2.refs_0_), channel_id=1, source_target_pairs={{0,16},{4,20},{8,24},{12,28},{16,0},{20,4},{24,8},{28,12},{1,17},{... | collective-permute-start | bytes 786440 | tf_op jit(solution)/shard_map/ppermute | solution.py:33
  41.9 23.5 %collective-permute-start.11 = (bf16[1024,128]{1,0:T(8,128)(2,1)S(1)}, bf16[1024,128]{1,0:T(8,128)(2,1)}, u32[]{:S(2)}, u32[]{:S(2)}) collective-permute-start(bf16[1024,128]{1,0:T(8,128)(2,1)S(1)} %pad_maximum_fusion.2.refs_0_), channel_id=1, source_target_pairs={{0,24},{4,28},{8,0},{12,4},{16,8},{20,12},{24,16},{28,20},{1,25},{... | collective-permute-start | bytes 786440 | tf_op jit(solution)/shard_map/ppermute | solution.py:33
  43.5 22.0 %collective-permute-start.13 = (bf16[1024,128]{1,0:T(8,128)(2,1)S(1)}, bf16[1024,128]{1,0:T(8,128)(2,1)}, u32[]{:S(2)}, u32[]{:S(2)}) collective-permute-start(bf16[1024,128]{1,0:T(8,128)(2,1)S(1)} %pad_maximum_fusion.2.refs_0_), channel_id=1, source_target_pairs={{0,8},{4,12},{8,16},{12,20},{16,24},{20,28},{24,0},{28,4},{1,9},{5... | collective-permute-start | bytes 786440 | tf_op jit(solution)/shard_map/ppermute | solution.py:33
  45.0 1.2 %copy-start.4 = (bf16[6272,128]{1,0:T(8,128)(2,1)}, bf16[6272,128]{1,0:T(8,128)(2,1)S(1)}, u32[]{:S(2)}) copy-start(bf16[6272,128]{1,0:T(8,128)(2,1)S(1)} %constant_dynamic-update-slice_fusion) | copy-start | bytes 4816900
  46.4 12.3 %collective-permute-start.10 = (bf16[2048,128]{1,0:T(8,128)(2,1)}, bf16[2048,128]{1,0:T(8,128)(2,1)}, u32[]{:S(2)}, u32[]{:S(2)}) collective-permute-start(bf16[2048,128]{1,0:T(8,128)(2,1)} %broadcast_select_fusion), channel_id=1, source_target_pairs={{0,4},{4,0},{8,12},{12,8},{16,20},{20,16},{24,28},{28,24},{1,5},{5... | collective-permute-start | bytes 1572872 | tf_op jit(solution)/shard_map/ppermute | solution.py:28
  50.2 15.2 %copy-start = (bf16[16,4,128,128]{3,2,1,0:T(8,128)(2,1)S(1)}, bf16[16,4,128,128]{3,2,1,0:T(8,128)(2,1)}, u32[]{:S(2)}) copy-start(bf16[16,4,128,128]{3,2,1,0:T(8,128)(2,1)} %prior.3) | copy-start | bytes 6291460

commit v4 on v3

--- a/solution.py
+++ b/solution.py
@@ -13,7 +13,7 @@
  'gates': {'Y1': ['Y0'], 'T': ['Z0'], 'I1': ['T'], 'I2': ['T'], 'E1': ['Y0'], 'E3': ['Y0']},
  'order': ['Z0', 'Z1', 'KM', 'T', 'I', 'X', 'Y0', 'Y1', 'E1', 'E2', 'E3'],
  'cost': 0,
- 'groups': 4,
+ 'groups': 2,
  'vmem': 48,
  'any': True,
  'parts_later': False}

time: 71.4 us -> 71.5 us (level)
  no operation moved by 1% of the time
where the time goes in v4:
time: 71.5 us; the launch traced here: 71.1 us
  waiting for transfers between devices  25.1 us (35%)
  starting transfers between devices  20.5 us (29%)
  Pallas kernels  13.4 us (19%)
  local copies, waits for them, and re-layouts  7.4 us (10%)
  other arithmetic  4.49 us (6%)
    ppermute x7, waiting for transfers between devices, taken_from(): lax.ppermute(array, axis, [(i, (i - ahead) % count) for i in range(count)])  16.7 us
    ppermute x7, starting transfers between devices, taken_from(): lax.ppermute(array, axis, [(i, (i - ahead) % count) for i in range(count)])  11.6 us
    ppermute x5, waiting for transfers between devices, exchange(): return lax.ppermute(array, axis, [(i, i ^ mask) for i in range(count)])  8.46 us
    pallas_call x1, Pallas kernels, local(): pl.pallas_call(functools.partial(left_kernel, tuple(layout), rows, per_qu...  6.07 us
    pallas_call x1, Pallas kernels, local(): pl.pallas_call(functools.partial(right_kernel, tuple(layout), rows, per_q...  5.66 us
    ppermute x5, starting transfers between devices, exchange(): return lax.ppermute(array, axis, [(i, i ^ mask) for i in range(count)])  4.25 us
    ppermute x1, starting transfers between devices, do_next(): w['kept'] = record('K', lax.ppermute(gated(parts[0], 'K'), both, kept))  3.31 us
    slice x1, local copies, waits for them, and re-layouts, local(): prior[half + starts[c]:half + starts[c] + sizes[c]].reshape(-1, block)  2.09 us
  transfers between devices with their start and end apart: 14, of which 4 were waited for; matrix products, arithmetic and copies ran while one was open for 13% of the time, Pallas kernels for 11%

profile of v4, /device:TPU:10, one launch (start us, length us, event | category | flops | bytes accessed | tf_op | source)
XLA Modules:
  0.0 71.1 jit_solution(5130459334286961082)
XLA Ops:
  0.0 1.0 %fusion.21 = (bf16[2,2,128,128]{3,2,1,0:T(8,128)(2,1)S(1)}, bf16[2,2,128,128]{3,2,1,0:T(8,128)(2,1)S(1)}) fusion(bf16[4,2,128,128]{3,2,1,0:T(8,128)(2,1)} %param.8), kind=kLoop, calls=%fused_computation.84 | loop fusion | bytes 524288 | tf_op jit(solution)/shard_map/slice | solution.py:203
  1.1 0.7 fusion.17
  1.7 0.1 slice_bitcast_fusion
  1.8 3.3 %collective-permute-start = (bf16[528,128]{1,0:T(8,128)(2,1)S(1)}, bf16[528,128]{1,0:T(8,128)(2,1)S(1)}, u32[]{:S(2)}, u32[]{:S(2)}) collective-permute-start(bf16[528,128]{1,0:T(8,128)(2,1)S(1)} %fusion.2), channel_id=1, source_target_pairs={{6,2},{7,3},{10,6},{11,7},{14,10},{15,11},{18,14},{19,15},{22,18},... | collective-permute-start | bytes 405512 | tf_op jit(solution)/shard_map/ppermute | solution.py:245
  5.2 1.3 %collective-permute-start.1 = (bf16[528,128]{1,0:T(8,128)(2,1)S(1)}, bf16[528,128]{1,0:T(8,128)(2,1)S(1)}, u32[]{:S(2)}, u32[]{:S(2)}) collective-permute-start(bf16[528,128]{1,0:T(8,128)(2,1)S(1)} %fusion.3), channel_id=1, source_target_pairs={{6,0},{7,1},{10,4},{11,5},{14,8},{15,9},{18,12},{19,13},{22,16},{2... | collective-permute-start | bytes 405512 | tf_op jit(solution)/shard_map/ppermute | solution.py:246
  6.5 2.1 %fusion.20 = (bf16[4,4,128,128]{3,2,1,0:T(8,128)(2,1)}, bf16[4,4,128,128]{3,2,1,0:T(8,128)(2,1)S(1)}) fusion(bf16[16,4,128,128]{3,2,1,0:T(8,128)(2,1)} %prior.3), kind=kLoop, calls=%fused_computation.83 | loop fusion | bytes 2097152 | tf_op jit(solution)/shard_map/slice | solution.py:197
  8.5 3.6 %collective-permute-start.4 = (bf16[2048,128]{1,0:T(8,128)(2,1)S(1)}, bf16[2048,128]{1,0:T(8,128)(2,1)S(1)}, u32[]{:S(2)}, u32[]{:S(2)}) collective-permute-start(bf16[2048,128]{1,0:T(8,128)(2,1)S(1)} %bitcast.25), channel_id=1, source_target_pairs={{0,24},{4,28},{8,0},{12,4},{16,8},{20,12},{24,16},{28,20},{1,25},{... | collective-permute-start | bytes 1572872 | tf_op jit(solution)/shard_map/ppermute | solution.py:33
  12.2 0.4 collective-permute-start.9
  12.6 0.7 %constant_dynamic-update-slice_fusion.4 = bf16[6272,128]{1,0:T(8,128)(2,1)} fusion(bf16[1024,128]{1,0:T(8,128)(2,1)S(1)} %bitcast.22), kind=kLoop, calls=%fused_computation.17 | loop fusion | bytes 524288
  13.4 0.1 iota_compare_fusion.4
  13.4 0.6 fusion.22
  14.2 0.1 slice.35
  14.2 1.6 %shard_map.55 = bf16[4,128,128]{2,1,0:T(8,128)(2,1)} custom-call(bf16[4,128,128]{2,1,0:T(8,128)(2,1)} %src.1), custom_call_target="tpu_custom_call" | custom-call | tf_op jit(solution)/shard_map/pallas_call | solution.py:210
  15.9 0.1 add.149
  16.0 0.1 copy.20
  16.0 0.1 reshape.196.index
  16.2 0.7 constant_dynamic-update-slice_fusion.2
  16.9 0.1 collective-permute-start.2
  17.0 8.3 %collective-permute-done.4.refs_5_ = bf16[2048,128]{1,0:T(8,128)(2,1)S(1)} collective-permute-done((bf16[2048,128]{1,0:T(8,128)(2,1)S(1)}, bf16[2048,128]{1,0:T(8,128)(2,1)S(1)}, u32[]{:S(2)}, u32[]{:S(2)}) %collective-permute-start.4) | collective-permute-done | bytes 524320 | tf_op jit(solution)/shard_map/ppermute | solution.py:33
  25.3 0.1 broadcast_select_fusion.1
  25.4 2.1 %collective-permute-start.8 = (bf16[2048,128]{1,0:T(8,128)(2,1)S(1)}, bf16[2048,128]{1,0:T(8,128)(2,1)S(1)}, u32[]{:S(2)}, u32[]{:S(2)}) collective-permute-start(bf16[2048,128]{1,0:T(8,128)(2,1)S(1)} %broadcast_select_fusion.1), channel_id=1, source_target_pairs={{0,4},{4,0},{8,12},{12,8},{16,20},{20,16},{24,28},{28,24},{1,5},{5... | collective-permute-start | bytes 1572872 | tf_op jit(solution)/shard_map/ppermute | solution.py:28
  27.5 0.1 collective-permute-start.3
  27.6 7.7 %collective-permute-done.9.refs_6_ = bf16[2048,128]{1,0:T(8,128)(2,1)S(1)} collective-permute-done((bf16[2048,128]{1,0:T(8,128)(2,1)}, bf16[2048,128]{1,0:T(8,128)(2,1)S(1)}, u32[]{:S(2)}, u32[]{:S(2)}) %collective-permute-start.9) | collective-permute-done | bytes 524320 | tf_op jit(solution)/shard_map/ppermute | solution.py:33
  35.4 1.9 %broadcast_select_fusion = bf16[2048,128]{1,0:T(8,128)(2,1)} fusion(bf16[2048,128]{1,0:T(8,128)(2,1)S(1)} %collective-permute-done.9.refs_6_, pred[]{:T(512)S(6)} %eq.123, bf16[4,4,128,128]{3,2,1,0:T(8,128)(2,1)} %get-tuple-element.19), kind=kLoop, calls=%fused_computation.1 | loop fusion | flops 262144 | bytes 1572865 | tf_op jit(solution)/shard_map/jit(_where)/select_n | solution.py:223
  37.4 3.7 %collective-permute-start.7 = (s32[8,4]{0,1:T(4,128)S(1)}, s32[8,4]{0,1:T(4,128)S(1)}, u32[]{:S(2)}, u32[]{:S(2)}) collective-permute-start(s32[8,4]{0,1:T(4,128)S(1)} %slice.35), channel_id=1, source_target_pairs={{0,24},{4,28},{8,0},{12,4},{16,8},{20,12},{24,16},{28,20},{1,25},{... | collective-permute-start | bytes 392 | tf_op jit(solution)/shard_map/ppermute | solution.py:33
  41.1 0.8 %collective-permute-start.12 = (bf16[1024,128]{1,0:T(8,128)(2,1)S(1)}, bf16[1024,128]{1,0:T(8,128)(2,1)}, u32[]{:S(2)}, u32[]{:S(2)}) collective-permute-start(bf16[1024,128]{1,0:T(8,128)(2,1)S(1)} %pad_maximum_fusion.2.refs_0_), channel_id=1, source_target_pairs={{0,16},{4,20},{8,24},{12,28},{16,0},{20,4},{24,8},{28,12},{1,17},{... | collective-permute-start | bytes 786440 | tf_op jit(solution)/shard_map/ppermute | solution.py:33
  41.9 1.5 %collective-permute-start.11 = (bf16[1024,128]{1,0:T(8,128)(2,1)S(1)}, bf16[1024,128]{1,0:T(8,128)(2,1)}, u32[]{:S(2)}, u32[]{:S(2)}) collective-permute-start(bf16[1024,128]{1,0:T(8,128)(2,1)S(1)} %pad_maximum_fusion.2.refs_0_), channel_id=1, source_target_pairs={{0,24},{4,28},{8,0},{12,4},{16,8},{20,12},{24,16},{28,20},{1,25},{... | collective-permute-start | bytes 786440 | tf_op jit(solution)/shard_map/ppermute | solution.py:33
  43.5 1.4 %collective-permute-start.13 = (bf16[1024,128]{1,0:T(8,128)(2,1)S(1)}, bf16[1024,128]{1,0:T(8,128)(2,1)}, u32[]{:S(2)}, u32[]{:S(2)}) collective-permute-start(bf16[1024,128]{1,0:T(8,128)(2,1)S(1)} %pad_maximum_fusion.2.refs_0_), channel_id=1, source_target_pairs={{0,8},{4,12},{8,16},{12,20},{16,24},{20,28},{24,0},{28,4},{1,9},{5... | collective-permute-start | bytes 786440 | tf_op jit(solution)/shard_map/ppermute | solution.py:33
  44.9 0.1 constant_dynamic-update-slice_fusion
  45.0 1.1 %copy-done.4 = bf16[6272,128]{1,0:T(8,128)(2,1)} copy-done((bf16[6272,128]{1,0:T(8,128)(2,1)}, bf16[6272,128]{1,0:T(8,128)(2,1)S(1)}, u32[]{:S(2)}) %copy-start.4) | copy-done | bytes 1605656
  46.2 0.1 select_reduce_fusion.2
  46.3 0.1 eq.108
  46.4 2.0 %collective-permute-start.10 = (bf16[2048,128]{1,0:T(8,128)(2,1)}, bf16[2048,128]{1,0:T(8,128)(2,1)}, u32[]{:S(2)}, u32[]{:S(2)}) collective-permute-start(bf16[2048,128]{1,0:T(8,128)(2,1)} %broadcast_select_fusion), channel_id=1, source_target_pairs={{0,4},{4,0},{8,12},{12,8},{16,20},{20,16},{24,28},{28,24},{1,5},{5... | collective-permute-start | bytes 1572872 | tf_op jit(solution)/shard_map/ppermute | solution.py:28
  48.4 0.1 select_reduce_fusion.1
  48.5 0.7 slice.40
  49.2 0.1 reshape.205
  49.3 0.2 select_reduce_fusion.3
  49.5 0.1 iota_compare_fusion.1
  49.6 0.1 copy.22
  49.7 0.1 select_n.177
  49.8 0.1 select_reduce_fusion
  50.0 0.1 copy.24
  50.1 0.1 select_n.182
  50.2 0.1 pad_add_fusion.index
  50.3 8.5 %collective-permute-done.10.refs_1_ = bf16[2048,128]{1,0:T(8,128)(2,1)} collective-permute-done((bf16[2048,128]{1,0:T(8,128)(2,1)}, bf16[2048,128]{1,0:T(8,128)(2,1)}, u32[]{:S(2)}, u32[]{:S(2)}) %collective-permute-start.10) | collective-permute-done | bytes 524320 | tf_op jit(solution)/shard_map/ppermute | solution.py:28
  58.7 6.1 %shard_map.56 = (bf16[16,128,512]{2,1,0:T(8,128)(2,1)S(1)}, bf16[16,128,512]{2,1,0:T(8,128)(2,1)}) custom-call(s32[120]{0:T(128)S(1)} %pad_add_fusion.index, bf16[16,4,128,128]{3,2,1,0:T(8,128)(2,1)} %prior.3, bf16[2048,128]{1,0:T(8,128)(2,1)S(1)} %collective-permute-done.8.refs_0_, bf16[2048,128]{1,0:T(8,128)(2,1)} %collective-permute-done.10.refs_1_, ...), custom_call_target="tpu_custom_call" | custom-call | bytes 8388608 | tf_op jit(solution)/shard_map/pallas_call | solution.py:364
  64.8 0.6 collective-permute-done.11.refs_1_
  65.4 5.7 %shard_map.57 = bf16[16,4,128,128]{3,2,1,0:T(8,128)(2,1)} custom-call(s32[64]{0:T(128)S(1)} %reshape.196.index, bf16[16,4,128,128]{3,2,1,0:T(8,128)(2,1)S(1)} %copy-done, bf16[16,128,512]{2,1,0:T(8,128)(2,1)S(1)} %get-tuple-element.14.first, bf16[16,128,512]{2,1,0:T(8,128)(2,1)} %get-tuple-element.15.second, ...), custom_call_target="tpu_custom_call" | custom-call | flops 1000000000 | bytes 8388608 | tf_op jit(solution)/shard_map/pallas_call | solution.py:389
  (50 shorter events, 0.6 us)
Async XLA Ops:
  0.0 12.6 %copy-start.1 = (bf16[4,2,128,128]{3,2,1,0:T(8,128)(2,1)S(1)}, bf16[4,2,128,128]{3,2,1,0:T(8,128)(2,1)}, u32[]{:S(2)}) copy-start(bf16[4,2,128,128]{3,2,1,0:T(8,128)(2,1)} %param.8) | copy-start | bytes 786436
  0.0 12.6 %copy-start.6 = (s32[4]{0:T(128)S(1)}, s32[4]{0:T(128)}, u32[]{:S(2)}) copy-start(s32[4]{0:T(128)} %param.7) | copy-start | bytes 52
  1.8 12.3 %copy-start.5 = (s32[16,4]{0,1:T(4,128)S(1)}, s32[16,4]{0,1:T(4,128)}, u32[]{:S(2)}) copy-start(s32[16,4]{0,1:T(4,128)} %param.6) | copy-start | bytes 772
  1.8 14.3 %collective-permute-start = (bf16[528,128]{1,0:T(8,128)(2,1)S(1)}, bf16[528,128]{1,0:T(8,128)(2,1)S(1)}, u32[]{:S(2)}, u32[]{:S(2)}) collective-permute-start(bf16[528,128]{1,0:T(8,128)(2,1)S(1)} %fusion.2), channel_id=1, source_target_pairs={{6,2},{7,3},{10,6},{11,7},{14,10},{15,11},{18,14},{19,15},{22,18},... | collective-permute-start | bytes 405512 | tf_op jit(solution)/shard_map/ppermute | solution.py:245
  5.2 11.0 %collective-permute-start.1 = (bf16[528,128]{1,0:T(8,128)(2,1)S(1)}, bf16[528,128]{1,0:T(8,128)(2,1)S(1)}, u32[]{:S(2)}, u32[]{:S(2)}) collective-permute-start(bf16[528,128]{1,0:T(8,128)(2,1)S(1)} %fusion.3), channel_id=1, source_target_pairs={{6,0},{7,1},{10,4},{11,5},{14,8},{15,9},{18,12},{19,13},{22,16},{2... | collective-permute-start | bytes 405512 | tf_op jit(solution)/shard_map/ppermute | solution.py:246
  8.5 16.7 %collective-permute-start.4 = (bf16[2048,128]{1,0:T(8,128)(2,1)S(1)}, bf16[2048,128]{1,0:T(8,128)(2,1)S(1)}, u32[]{:S(2)}, u32[]{:S(2)}) collective-permute-start(bf16[2048,128]{1,0:T(8,128)(2,1)S(1)} %bitcast.25), channel_id=1, source_target_pairs={{0,24},{4,28},{8,0},{12,4},{16,8},{20,12},{24,16},{28,20},{1,25},{... | collective-permute-start | bytes 1572872 | tf_op jit(solution)/shard_map/ppermute | solution.py:33
  12.2 23.2 %collective-permute-start.9 = (bf16[2048,128]{1,0:T(8,128)(2,1)}, bf16[2048,128]{1,0:T(8,128)(2,1)S(1)}, u32[]{:S(2)}, u32[]{:S(2)}) collective-permute-start(bf16[2048,128]{1,0:T(8,128)(2,1)} %bitcast.10), channel_id=1, source_target_pairs={{0,24},{4,28},{8,0},{12,4},{16,8},{20,12},{24,16},{28,20},{1,25},{... | collective-permute-start | bytes 1572872 | tf_op jit(solution)/shard_map/ppermute | solution.py:33
  16.9 10.6 %collective-permute-start.2 = (bf16[1568,128]{1,0:T(8,128)(2,1)S(1)}, bf16[1568,128]{1,0:T(8,128)(2,1)S(1)}, u32[]{:S(2)}, u32[]{:S(2)}) collective-permute-start(bf16[1568,128]{1,0:T(8,128)(2,1)S(1)} %pad_maximum_fusion.1.refs_2_), channel_id=1, source_target_pairs={{0,2},{1,3},{2,0},{3,1},{4,6},{5,7},{6,4},{7,5},{8,10},{9,11},{10,... | collective-permute-start | bytes 1204232 | tf_op jit(solution)/shard_map/ppermute | solution.py:28
  25.3 12.0 %collective-permute-start.5 = (bf16[512,128]{1,0:T(8,128)(2,1)}, bf16[512,128]{1,0:T(8,128)(2,1)S(1)}, u32[]{:S(2)}, u32[]{:S(2)}) collective-permute-start(bf16[512,128]{1,0:T(8,128)(2,1)} %bitcast.26), channel_id=1, source_target_pairs={{0,4},{4,0},{8,12},{12,8},{16,20},{20,16},{24,28},{28,24},{1,5},{5... | collective-permute-start | bytes 393224 | tf_op jit(solution)/shard_map/ppermute | solution.py:28
  25.4 11.9 %copy-start.3 = (bf16[6272,128]{1,0:T(8,128)(2,1)S(1)}, bf16[6272,128]{1,0:T(8,128)(2,1)}, u32[]{:S(2)}) copy-start(bf16[6272,128]{1,0:T(8,128)(2,1)} %get-tuple-element.17) | copy-start | bytes 4816900
  25.4 15.7 %copy-start.2 = (bf16[4,128,128]{2,1,0:T(8,128)(2,1)S(1)}, bf16[4,128,128]{2,1,0:T(8,128)(2,1)}, u32[]{:S(2)}) copy-start(bf16[4,128,128]{2,1,0:T(8,128)(2,1)} %shard_map.55) | copy-start | bytes 393220
  25.4 16.6 %collective-permute-start.8 = (bf16[2048,128]{1,0:T(8,128)(2,1)S(1)}, bf16[2048,128]{1,0:T(8,128)(2,1)S(1)}, u32[]{:S(2)}, u32[]{:S(2)}) collective-permute-start(bf16[2048,128]{1,0:T(8,128)(2,1)S(1)} %broadcast_select_fusion.1), channel_id=1, source_target_pairs={{0,4},{4,0},{8,12},{12,8},{16,20},{20,16},{24,28},{28,24},{1,5},{5... | collective-permute-start | bytes 1572872 | tf_op jit(solution)/shard_map/ppermute | solution.py:28
  27.5 15.9 %collective-permute-start.3 = (bf16[3136,128]{1,0:T(8,128)(2,1)S(1)}, bf16[3136,128]{1,0:T(8,128)(2,1)S(1)}, u32[]{:S(2)}, u32[]{:S(2)}) collective-permute-start(bf16[3136,128]{1,0:T(8,128)(2,1)S(1)} %pad_maximum_fusion), channel_id=1, source_target_pairs={{0,1},{1,0},{2,3},{3,2},{4,5},{5,4},{6,7},{7,6},{8,9},{9,8},{10,11... | collective-permute-start | bytes 2408456 | tf_op jit(solution)/shard_map/ppermute | solution.py:28
  37.3 9.1 %collective-permute-start.6 = (s32[8,4]{0,1:T(4,128)S(1)}, s32[8,4]{0,1:T(4,128)S(1)}, u32[]{:S(2)}, u32[]{:S(2)}) collective-permute-start(s32[8,4]{0,1:T(4,128)S(1)} %slice.35), channel_id=1, source_target_pairs={{0,28},{4,0},{8,4},{12,8},{16,12},{20,16},{24,20},{28,24},{1,29},{... | collective-permute-start | bytes 392 | tf_op jit(solution)/shard_map/ppermute | solution.py:33
  37.4 12.4 %collective-permute-start.7 = (s32[8,4]{0,1:T(4,128)S(1)}, s32[8,4]{0,1:T(4,128)S(1)}, u32[]{:S(2)}, u32[]{:S(2)}) collective-permute-start(s32[8,4]{0,1:T(4,128)S(1)} %slice.35), channel_id=1, source_target_pairs={{0,24},{4,28},{8,0},{12,4},{16,8},{20,12},{24,16},{28,20},{1,25},{... | collective-permute-start | bytes 392 | tf_op jit(solution)/shard_map/ppermute | solution.py:33
  41.1 23.7 %collective-permute-start.12 = (bf16[1024,128]{1,0:T(8,128)(2,1)S(1)}, bf16[1024,128]{1,0:T(8,128)(2,1)}, u32[]{:S(2)}, u32[]{:S(2)}) collective-permute-start(bf16[1024,128]{1,0:T(8,128)(2,1)S(1)} %pad_maximum_fusion.2.refs_0_), channel_id=1, source_target_pairs={{0,16},{4,20},{8,24},{12,28},{16,0},{20,4},{24,8},{28,12},{1,17},{... | collective-permute-start | bytes 786440 | tf_op jit(solution)/shard_map/ppermute | solution.py:33
  41.9 23.5 %collective-permute-start.11 = (bf16[1024,128]{1,0:T(8,128)(2,1)S(1)}, bf16[1024,128]{1,0:T(8,128)(2,1)}, u32[]{:S(2)}, u32[]{:S(2)}) collective-permute-start(bf16[1024,128]{1,0:T(8,128)(2,1)S(1)} %pad_maximum_fusion.2.refs_0_), channel_id=1, source_target_pairs={{0,24},{4,28},{8,0},{12,4},{16,8},{20,12},{24,16},{28,20},{1,25},{... | collective-permute-start | bytes 786440 | tf_op jit(solution)/shard_map/ppermute | solution.py:33
  43.5 22.0 %collective-permute-start.13 = (bf16[1024,128]{1,0:T(8,128)(2,1)S(1)}, bf16[1024,128]{1,0:T(8,128)(2,1)}, u32[]{:S(2)}, u32[]{:S(2)}) collective-permute-start(bf16[1024,128]{1,0:T(8,128)(2,1)S(1)} %pad_maximum_fusion.2.refs_0_), channel_id=1, source_target_pairs={{0,8},{4,12},{8,16},{12,20},{16,24},{20,28},{24,0},{28,4},{1,9},{5... | collective-permute-start | bytes 786440 | tf_op jit(solution)/shard_map/ppermute | solution.py:33
  45.0 1.2 %copy-start.4 = (bf16[6272,128]{1,0:T(8,128)(2,1)}, bf16[6272,128]{1,0:T(8,128)(2,1)S(1)}, u32[]{:S(2)}) copy-start(bf16[6272,128]{1,0:T(8,128)(2,1)S(1)} %constant_dynamic-update-slice_fusion) | copy-start | bytes 4816900
  46.4 12.3 %collective-permute-start.10 = (bf16[2048,128]{1,0:T(8,128)(2,1)}, bf16[2048,128]{1,0:T(8,128)(2,1)}, u32[]{:S(2)}, u32[]{:S(2)}) collective-permute-start(bf16[2048,128]{1,0:T(8,128)(2,1)} %broadcast_select_fusion), channel_id=1, source_target_pairs={{0,4},{4,0},{8,12},{12,8},{16,20},{20,16},{24,28},{28,24},{1,5},{5... | collective-permute-start | bytes 1572872 | tf_op jit(solution)/shard_map/ppermute | solution.py:28
  50.2 15.2 %copy-start = (bf16[16,4,128,128]{3,2,1,0:T(8,128)(2,1)S(1)}, bf16[16,4,128,128]{3,2,1,0:T(8,128)(2,1)}, u32[]{:S(2)}) copy-start(bf16[16,4,128,128]{3,2,1,0:T(8,128)(2,1)} %prior.3) | copy-start | bytes 6291460
